TPU v7x, 256 devices: a whole 4x4x8 slice. The times are simulated.
256 devices in a mesh: segment: 4 (over y), dom: 64 (over x, z, core).
Axes of the slice: x: 4, y: 4, z: 8, core: 2. Of those that a mesh axis runs over, the one named last changes fastest.
Arguments:
- forward_held: float32 [4, 16384, 512], P('segment', 'dom'), may hold values from -6 to 6
- forward_new: float32 [16384, 512], P('dom'), may hold values from -6 to 6
- back_outputs: float32 [4, 16384, 512], P('segment', 'dom'), may hold values from -6 to 6
- back_cotangents: float32 [4, 16384, 512], P('segment', 'dom'), may hold values from -6 to 6
- back_new_outputs: float32 [16384, 512], P('dom'), may hold values from -6 to 6
- back_new_cotangents: float32 [16384, 512], P('dom'), may hold values from -6 to 6
- adj_tiles: float32 [128, 16, 128, 128], P('dom'), may hold values from 0 to 0.046875, as said below
- tile_cols: int32 [128, 16], P('dom'), may hold values from 0 to 127, as said below
- weight_first: float32 [8, 256, 256], P('segment'), may hold values from -0.375 to 0.375
- weight_second: float32 [8, 256, 256], P('segment'), may hold values from -0.375 to 0.375
- gain_first: float32 [8, 256], P('segment'), may hold values from 0.1 to 1.9
- gain_second: float32 [8, 256], P('segment'), may hold values from 0.1 to 1.9
Outputs:
- forward_one: float32 [4, 16384, 512], P('segment', 'dom')
- forward_two: float32 [4, 16384, 512], P('segment', 'dom')
- inputs_one: float32 [4, 16384, 512], P('segment', 'dom')
- cotan_one: float32 [4, 16384, 512], P('segment', 'dom')
- inputs_two: float32 [4, 16384, 512], P('segment', 'dom')
- cotan_two: float32 [4, 16384, 512], P('segment', 'dom')
- grad_weight_first: float32 [8, 256, 256], P('segment')
- grad_weight_second: float32 [8, 256, 256], P('segment')
- grad_gain_first: float32 [8, 256], P('segment')
- grad_gain_second: float32 [8, 256], P('segment')
Inputs may be any that keep to these rules, and one draw needn't show every extreme that they name: tile_cols[r, t] lies between max(0, (r // 2 - 1) * 2) and min(128, (r // 2 + 2) * 2) - 1: a block of the row block's own partition or of the partition on either side; a column block may appear several times in a row. `adj_tiles`: each entry is zero or positive; a node's row over its 16 tiles holds about 32 nonzero entries, and its expected sum is one.
All inputs are finite; a program needn't handle non-finite values.
Results may differ from a plain program's by a relative error of at most 0.00085.
Values sent between devices are 32-bit elements; how exact they have to be, the bound alone decides.
No kernel may reach another device: no remote copies, remote signals or barrier semaphores. Data moves between devices by JAX's collectives and lax.ppermute only.
A program may use at most 128 MiB of HBM per device.

v0:
```python
import functools
import math

import jax
import jax.numpy as jnp
from jax import lax
from jax.experimental import pallas as pl
from jax.experimental.pallas import tpu as pltpu
from jax.sharding import PartitionSpec as P

F32 = jnp.float32
BF16 = jnp.bfloat16
N = 256
BLOCK = 128
TILES = 16
LAYERS = 2
FIRST, SECOND = 0, 1
A, B, C = slice(0, N), slice(N, 2 * N), slice(2 * N, 3 * N)


def split(x):
    hi = x.astype(BF16)
    return hi, (x - hi.astype(F32)).astype(BF16)


def split3(x):
    hi = x.astype(BF16)
    rest = x - hi.astype(F32)
    mid = rest.astype(BF16)
    return hi, mid, (rest - mid.astype(F32)).astype(BF16)


def mm(a, b):
    return jnp.dot(a, b, preferred_element_type=F32)


def dot3(a, b):
    return mm(a[0], b[0]) + (mm(a[0], b[1]) + mm(a[1], b[0]))


def dot6(a, b):
    small = mm(a[0], b[2]) + (mm(a[2], b[0]) + mm(a[1], b[1]))
    return mm(a[0], b[0]) + ((mm(a[0], b[1]) + mm(a[1], b[0])) + small)


def norm(h):
    centred = h - jnp.mean(h, axis=1, keepdims=True)
    rstd = lax.rsqrt(jnp.mean(centred * centred, axis=1, keepdims=True) + 1e-05)
    return centred * rstd, rstd


def active(h, gain):
    return jnp.maximum(norm(h)[0] * gain, 0.0)


def at(branch, l):
    return branch * LAYERS + l


def half(array, j):
    return array, pl.BlockSpec((N, N), lambda i: (0, j))


def run(kernel, outs, *operands, flops=0, scratch=()):
    arrays, specs = [], []
    for o in operands:
        pair = isinstance(o, tuple)
        arrays.append(o[0] if pair else o)
        specs.append(o[1] if pair else pl.BlockSpec(memory_space=pltpu.VMEM))
    return pl.pallas_call(
        kernel,
        out_shape=[jax.ShapeDtypeStruct(s, t) for s, t in outs],
        grid=(1,),
        in_specs=specs,
        out_specs=[pl.BlockSpec(memory_space=pltpu.VMEM)] * len(outs),
        scratch_shapes=list(scratch),
        compiler_params=pltpu.CompilerParams(vmem_limit_bytes=12 << 20),
        cost_estimate=pl.CostEstimate(flops=flops, bytes_accessed=1024, transcendentals=0),
    )(*arrays)


MAT = ((N, N), F32)
PAIR = ((2 * N, N), F32)
PACK = ((3 * N, N), F32)
FULL = ((N, 2 * N), F32)
THIN = ((N, BLOCK), F32)
PRODUCT = 1024


def band_kernel(tiles, cols, band, across, acc):
    dom = lax.axis_index("dom")
    parity = lax.rem(dom, 2)
    first = (dom - 1) * 2
    acc[...] = jnp.zeros_like(acc)
    for r in range(2):
        for t in range(TILES):
            place = cols[r, t] - first
            group = place // 2
            side = jnp.where(group == 2, 1, 0)
            which = jnp.where(group == 1, 0, jnp.where(side == parity, 2, 1))
            acc[r * 6 + which * 2 + (place - group * 2)] += tiles[r, t]
    for r in range(2):
        rows = slice(r * BLOCK, (r + 1) * BLOCK)
        for c in range(6):
            columns = slice(c * BLOCK, (c + 1) * BLOCK)
            block = acc[r * 6 + c]
            for i, piece in enumerate(split3(block)):
                band[i, rows, columns] = piece
            for i, piece in enumerate(split(block.T)):
                across[i, columns, rows] = piece


def weight_kernel(first, second, gain_first, gain_second, gains, weights, turned):
    for branch, (w, gain) in enumerate([(first, gain_first), (second, gain_second)]):
        for l in range(LAYERS):
            k = at(branch, l)
            gains[k : k + 1, :] = gain[l : l + 1, :]
            value = w[l]
            for i, piece in enumerate(split3(value)):
                weights[i, k] = piece
            for i, piece in enumerate(split(value.T)):
                turned[i, k] = piece


def pieces(ref, *where, count):
    return [ref[(i, *where)] for i in range(count)]


def mixed6(h, k, gains, weights):
    return dot6(split3(active(h, gains[k : k + 1, :])), pieces(weights, k, count=3))


def mixed3(h, k, gains, weights):
    return dot3(split(active(h, gains[k : k + 1, :])), pieces(weights, k, count=2))


def aggregate6(band, columns, values):
    return dot6(pieces(band, slice(0, N), columns, count=3), split3(values))


def aggregate3(band, columns, values):
    return dot3(pieces(band, slice(0, N), columns, count=2), split(values))


def owed_to(across, rows, g):
    return dot3(pieces(across, rows, slice(0, N), count=2), split(g))


def pulled(k, xhat, rstd, back, target, gains, turned):
    scale = gains[k : k + 1, :]
    grown = dot3(split(back), pieces(turned, k, count=2))
    dxhat = jnp.where(xhat * scale > 0.0, grown, 0.0) * scale
    inner = jnp.mean(dxhat * xhat, axis=1, keepdims=True)
    return target + rstd * (dxhat - jnp.mean(dxhat, axis=1, keepdims=True) - xhat * inner)


def weight_grad(k, xhat, back, gains):
    act = jnp.maximum(xhat * gains[k : k + 1, :], 0.0)
    return dot3(split(act.T), split(back))


def entry_kernel(l, y1, g2, x2, across, gain_second, weight_second, gain_first, weight_first, sent):
    act = active(y1[...], gain_second[l : l + 1, :])
    sent[A, :] = dot6(split3(act), split3(weight_second[l]))
    sent[B, :] = owed_to(across, C, g2[...])
    act = active(x2[...], gain_first[0:1, :])
    sent[C, :] = dot3(split(act), split(weight_first[0]))


def next_kernel(
    k, y_new, g_new, x_new, early, late, ahead, across, gains, weights,
    y1, y2, g1, g2, x1, x2, sent,
):
    segment = lax.axis_index("segment")
    is_last = segment == lax.axis_size("segment") - 1
    is_first = segment == 0
    upper = jnp.where(is_last, y_new[:, A], late[A, :])
    lower_cot = jnp.where(is_last, g_new[:, B], late[B, :])
    lower = jnp.where(is_first, x_new[:, B], ahead[B, :])
    sent[A, :] = mixed6(upper, k, gains, weights)
    sent[B, :] = owed_to(across, C, lower_cot)
    sent[C, :] = mixed3(lower, at(FIRST, 0), gains, weights)
    y1[...] = upper
    g2[...] = lower_cot
    x2[...] = lower
    y2[...] = jnp.where(is_last, y_new[:, B], early[A, :])
    g1[...] = jnp.where(is_last, g_new[:, A], early[B, :])
    x1[...] = jnp.where(is_first, x_new[:, A], ahead[A, :])


def local_kernel(sent, target, g, x, band, across, inverse, owed, forward, sib, sib_owed):
    mixed, fed = sent[A, :], sent[C, :]
    value = g[...]
    sib[A, :] = mixed
    sib[B, :] = fed
    sib_owed[...] = owed_to(across, B, value)
    owed[...] = owed_to(across, A, value)
    inverse[...] = target[...] - aggregate6(band, A, mixed)
    forward[...] = x[...] + aggregate3(band, A, fed)


def near_kernel(
    inverse, owed, forward, near, near_owed, h, band, inverse_out, owed_out, forward_out, xhat, rstd
):
    inverse_out[...] = inverse[...] - aggregate6(band, B, near[A, :])
    owed_out[...] = owed[...] + near_owed[...]
    forward_out[...] = forward[...] + aggregate3(band, B, near[B, :])
    normed, scale = norm(h[...])
    xhat[...] = normed
    rstd[...] = jnp.broadcast_to(scale, rstd.shape)


def joined(k, inverse, owed, forward, far, xhat, rstd, cot, band, gains, turned):
    value = inverse[...] - aggregate6(band, C, far[A, :])
    back = owed[...] + far[B, :]
    carried = pulled(k, xhat[...], rstd[:, 0:1], back, cot[...], gains, turned)
    ahead = forward[...] + aggregate3(band, C, far[C, :])
    return value, back, carried, ahead


def join_kernel(
    k, inverse_k, forward_k, inverse, owed, forward, far, xhat, rstd, cot, band, gains, turned,
    across, weights, value_out, carried_out, ahead_out, back_out, sent, *packed,
):
    value, back, carried, ahead = joined(
        k, inverse, owed, forward, far, xhat, rstd, cot, band, gains, turned
    )
    sent[A, :] = mixed6(value, inverse_k, gains, weights)
    sent[B, :] = owed_to(across, C, carried)
    sent[C, :] = mixed3(ahead, forward_k, gains, weights)
    value_out[...] = value
    carried_out[...] = carried
    ahead_out[...] = ahead
    back_out[...] = back
    if packed:
        packed[0][A, :] = value
        packed[0][B, :] = carried


def grad_kernel(k, xhat, back, gains, *refs):
    value = weight_grad(k, xhat[...], back[...], gains)
    refs[-1][...] = value + refs[0][...] if len(refs) > 1 else value


def last_kernel(
    final, k, inverse, owed, forward, far, xhat, rstd, cot, band, gains, turned, low, top_cot, top,
    *refs,
):
    if final:
        before, first_high, second_low, second_high, *refs = refs
    whole, whole_cot, whole_ahead, *refs = refs
    value, back, carried, ahead = joined(
        k, inverse, owed, forward, far, xhat, rstd, cot, band, gains, turned
    )
    whole[:, A] = value
    whole[:, B] = low[...]
    whole_cot[:, A] = top_cot[...]
    whole_cot[:, B] = carried
    whole_ahead[:, A] = top[...]
    whole_ahead[:, B] = ahead
    if final:
        keep, give = refs
        grad = before[...] + weight_grad(k, xhat[...], back, gains)
        even = lax.rem(lax.axis_index("dom"), 2) == 0
        keep[A, :] = jnp.where(even, grad, second_low[...])
        keep[B, :] = jnp.where(even, first_high[...], second_high[...])
        give[A, :] = jnp.where(even, second_low[...], grad)
        give[B, :] = jnp.where(even, second_high[...], first_high[...])
    else:
        back_out, late, ahead_out = refs
        back_out[...] = back
        late[A, :] = value
        late[B, :] = carried
        ahead_out[A, :] = top[...]
        ahead_out[B, :] = ahead


def add_kernel(a, b, out):
    out[...] = a[...] + b[...]


def share_kernel(scale, parts, out):
    total = jnp.sum(parts[...], axis=0) * scale
    out[...] = jnp.broadcast_to(total[None], out.shape)


def finish_kernel(
    mine, theirs, weight_first, weight_second, gain_first, gain_second, first, second, dgf, dgs
):
    even = lax.rem(lax.axis_index("dom"), 2) == 0
    a = mine[...]
    b = theirs[...]
    wf = jnp.where(even, a, b).reshape(first.shape)
    ws = jnp.where(even, b, a).reshape(second.shape)
    first[...] = wf
    second[...] = ws
    dgf[...] = jnp.sum(wf * weight_first[...], axis=2) / gain_first[...]
    dgs[...] = jnp.sum(ws * weight_second[...], axis=2) / gain_second[...]


def per_device(
    forward_held,
    forward_new,
    back_outputs,
    back_cotangents,
    back_new_outputs,
    back_new_cotangents,
    adj_tiles,
    tile_cols,
    weight_first,
    weight_second,
    gain_first,
    gain_second,
):
    dom_count = lax.axis_size("dom")
    last = lax.axis_size("segment") - 1
    top_layer = LAYERS - 1
    up = [(i, i + 1) for i in range(1, dom_count - 1, 2)]
    far_pairs = up + [(j, i) for i, j in up]
    sib_pairs = [(i, i ^ 1) for i in range(dom_count)]

    def far(v):
        return lax.ppermute(v, "dom", far_pairs)

    def near(v):
        return lax.ppermute(v, "dom", sib_pairs)

    def onward(v):
        return lax.ppermute(v, "segment", [(i, i + 1) for i in range(last)])

    def backward(v):
        return lax.ppermute(v, "segment", [(i + 1, i) for i in range(last)])

    part = functools.partial
    band, across = run(
        band_kernel,
        [((3, N, 3 * N), BF16), ((2, 3 * N, N), BF16)],
        adj_tiles,
        (tile_cols, pl.BlockSpec(memory_space=pltpu.SMEM)),
        scratch=[pltpu.VMEM((12, BLOCK, BLOCK), F32)],
        flops=PRODUCT,
    )
    gains, weights, turned = run(
        weight_kernel,
        [((2 * LAYERS, N), F32), ((3, 2 * LAYERS, N, N), BF16), ((2, 2 * LAYERS, N, N), BF16)],
        weight_first, weight_second, gain_first, gain_second, flops=PRODUCT,
    )
    out, cot, held = back_outputs[0], back_cotangents[0], forward_held[0]
    y1, y2, g1, g2 = half(out, 0), half(out, 1), half(cot, 0), half(cot, 1)
    x1, x2 = half(held, 0), half(held, 1)
    sent = run(
        part(entry_kernel, top_layer), [PACK], y1, g2, x2, across, gain_second, weight_second,
        gain_first, weight_first, flops=3 * PRODUCT,
    )[0]
    grads, results = {}, []
    for slot in range(2):
        for step in range(2 * LAYERS):
            even = step % 2 == 0
            l = top_layer - step // 2
            k = at(SECOND if even else FIRST, l)
            target, h, g, cot, x = (y2, y1, g2, g1, x1) if even else (y1, y2, g1, g2, x2)
            from_far = far(sent)
            inverse, owed, forward, sib, sib_owed = run(
                local_kernel, [MAT, MAT, MAT, PAIR, MAT], sent, target, g, x, band, across,
                flops=4 * PRODUCT,
            )
            from_near = (near(sib), near(sib_owed))
            inverse, owed, forward, xhat, rstd = run(
                near_kernel, [MAT, MAT, MAT, MAT, THIN], inverse, owed, forward, *from_near, h, band,
                flops=3 * PRODUCT,
            )
            operands = (inverse, owed, forward, from_far, xhat, rstd, cot, band, gains, turned)
            if step < 2 * LAYERS - 1:
                inverse_k = at(FIRST, l) if even else at(SECOND, l - 1)
                forward_k = at(SECOND, step // 2) if even else at(FIRST, step // 2 + 1)
                packed = [PAIR] if slot == 0 and step == 2 * LAYERS - 2 else []
                value, carried, ahead, back, sent, *packed = run(
                    part(join_kernel, k, inverse_k, forward_k), [MAT, MAT, MAT, MAT, PACK] + packed,
                    *operands, across, weights, flops=6 * PRODUCT,
                )
                if even:
                    y2, g1, x1 = value, carried, ahead
                else:
                    y1, g2, x2 = value, carried, ahead
                if packed:
                    early = backward(packed[0])
            elif slot == 0:
                *wholes, back, late, onwards = run(
                    part(last_kernel, False, k), [FULL, FULL, FULL, MAT, PAIR, PAIR], *operands, y2,
                    g1, x1, flops=4 * PRODUCT,
                )
                late, onwards = backward(late), onward(onwards)
            else:
                *wholes, keep, give = run(
                    part(last_kernel, True, k), [FULL, FULL, FULL, PAIR, PAIR], *operands, y2, g1,
                    x1, grads[at(FIRST, 0)], grads[at(FIRST, 1)], grads[at(SECOND, 0)],
                    grads[at(SECOND, 1)], flops=5 * PRODUCT,
                )
                break
            before = [grads[k]] if k in grads else []
            grads[k] = run(part(grad_kernel, k), [MAT], xhat, back, gains, *before, flops=PRODUCT)[0]
        results.append(wholes)
        if slot == 0:
            y1, y2, g1, g2, x1, x2, sent = run(
                part(next_kernel, at(SECOND, top_layer)), [MAT] * 6 + [PACK], back_new_outputs,
                back_new_cotangents, forward_new, early, late, onwards, across, gains, weights,
                flops=3 * PRODUCT,
            )

    groups = [list(range(c, dom_count, 2)) for c in range(2)]
    chips = dom_count // 2
    shares = (chips, LAYERS * N // chips, N)

    def exchanged(v):
        return lax.all_to_all(v, "dom", 0, 0, axis_index_groups=groups, tiled=True)

    summed = run(add_kernel, [PAIR], keep, near(give))[0]
    parts = exchanged(summed.reshape(shares))
    scale_factor = 1.0 / math.sqrt(2.0 * N * dom_count)
    mine = exchanged(run(part(share_kernel, scale_factor), [(shares, F32)], parts)[0])
    mine = mine.reshape(LAYERS * N, N)
    square, line = ((LAYERS, N, N), F32), ((LAYERS, N), F32)
    finals = run(
        finish_kernel, [square, square, line, line], mine, near(mine), weight_first, weight_second,
        gain_first, gain_second,
    )
    (inputs_a, cotan_a, ahead_a), (inputs_b, cotan_b, ahead_b) = results
    nodes = (ahead_a, ahead_b, inputs_a, cotan_a, inputs_b, cotan_b)
    return tuple(v[None] for v in nodes) + tuple(finals)


def solution(mesh):
    rows = P("segment", "dom", None)
    nodes = P("dom", None)
    weights = P("segment", None, None)
    gains = P("segment", None)
    return jax.shard_map(
        per_device,
        mesh=mesh,
        in_specs=(
            rows,
            nodes,
            rows,
            rows,
            nodes,
            nodes,
            P("dom", None, None, None),
            nodes,
            weights,
            weights,
            gains,
            gains,
        ),
        out_specs=(rows,) * 6 + (weights, weights, gains, gains),
        check_vma=False,
    )
```

profile of v0, /device:TPU:1, one launch (start us, length us, event | category | flops | bytes accessed | tf_op | source)
XLA Modules:
  0.0 210.9 jit_solution(13281354865331342574)
XLA Ops:
  6.2 4.9 %collective-permute-start.2 = (f32[768,256]{1,0:T(8,128)S(1)}, f32[768,256]{1,0:T(8,128)S(1)}, u32[]{:S(2)}, u32[]{:S(2)}) collective-permute-start(f32[768,256]{1,0:T(8,128)S(1)} %shard_map.196.sent), channel_id=1, source_target_pairs={{1,2},{3,4},{5,6},{7,8},{9,10},{11,12},{13,14},{15,16},{17,18},{19... | collective-permute-start | bytes 2359304 | tf_op jit(solution)/shard_map/ppermute | solution.py:323
  14.8 6.0 %collective-permute-done.2.far = f32[768,256]{1,0:T(8,128)S(1)} collective-permute-done((f32[768,256]{1,0:T(8,128)S(1)}, f32[768,256]{1,0:T(8,128)S(1)}, u32[]{:S(2)}, u32[]{:S(2)}) %collective-permute-start.2) | collective-permute-done | bytes 786464 | tf_op jit(solution)/shard_map/ppermute | solution.py:323
  22.2 3.6 %collective-permute-start.5 = (f32[768,256]{1,0:T(8,128)S(1)}, f32[768,256]{1,0:T(8,128)S(1)}, u32[]{:S(2)}, u32[]{:S(2)}) collective-permute-start(f32[768,256]{1,0:T(8,128)S(1)} %get-tuple-element.163.sent), channel_id=1, source_target_pairs={{1,2},{3,4},{5,6},{7,8},{9,10},{11,12},{13,14},{15,16},{17,18},{19... | collective-permute-start | bytes 2359304 | tf_op jit(solution)/shard_map/ppermute | solution.py:323
  27.2 1.8 collective-permute-done.4.near_owed
  29.5 6.0 %collective-permute-done.5.far = f32[768,256]{1,0:T(8,128)S(1)} collective-permute-done((f32[768,256]{1,0:T(8,128)S(1)}, f32[768,256]{1,0:T(8,128)S(1)}, u32[]{:S(2)}, u32[]{:S(2)}) %collective-permute-start.5) | collective-permute-done | bytes 786464 | tf_op jit(solution)/shard_map/ppermute | solution.py:323
  36.8 3.6 %collective-permute-start.8 = (f32[768,256]{1,0:T(8,128)S(1)}, f32[768,256]{1,0:T(8,128)S(1)}, u32[]{:S(2)}, u32[]{:S(2)}) collective-permute-start(f32[768,256]{1,0:T(8,128)S(1)} %get-tuple-element.176.sent), channel_id=1, source_target_pairs={{1,2},{3,4},{5,6},{7,8},{9,10},{11,12},{13,14},{15,16},{17,18},{19... | collective-permute-start | bytes 2359304 | tf_op jit(solution)/shard_map/ppermute | solution.py:323
  44.1 6.0 %collective-permute-done.8.far = f32[768,256]{1,0:T(8,128)S(1)} collective-permute-done((f32[768,256]{1,0:T(8,128)S(1)}, f32[768,256]{1,0:T(8,128)S(1)}, u32[]{:S(2)}, u32[]{:S(2)}) %collective-permute-start.8) | collective-permute-done | bytes 786464 | tf_op jit(solution)/shard_map/ppermute | solution.py:323
  51.5 3.8 %collective-permute-start.11 = (f32[768,256]{1,0:T(8,128)S(1)}, f32[768,256]{1,0:T(8,128)S(1)}, u32[]{:S(2)}, u32[]{:S(2)}) collective-permute-start(f32[768,256]{1,0:T(8,128)S(1)} %get-tuple-element.190.sent), channel_id=1, source_target_pairs={{1,2},{3,4},{5,6},{7,8},{9,10},{11,12},{13,14},{15,16},{17,18},{19... | collective-permute-start | bytes 2359304 | tf_op jit(solution)/shard_map/ppermute | solution.py:323
  58.9 6.2 %collective-permute-done.11.far = f32[768,256]{1,0:T(8,128)S(1)} collective-permute-done((f32[768,256]{1,0:T(8,128)S(1)}, f32[768,256]{1,0:T(8,128)S(1)}, u32[]{:S(2)}, u32[]{:S(2)}) %collective-permute-start.11) | collective-permute-done | bytes 786464 | tf_op jit(solution)/shard_map/ppermute | solution.py:323
  68.1 4.0 %collective-permute-start.14 = (f32[512,256]{1,0:T(8,128)S(1)}, f32[512,256]{1,0:T(8,128)S(1)}, u32[]{:S(2)}, u32[]{:S(2)}) collective-permute-start(f32[512,256]{1,0:T(8,128)S(1)} %get-tuple-element.208), channel_id=1, source_target_pairs={{0,64},{64,128},{128,192},{1,65},{65,129},{129,193},{2,66},{66,130... | collective-permute-start | bytes 1572872 | tf_op jit(solution)/shard_map/ppermute | solution.py:329
  72.1 11.1 %collective-permute-done.13.late = f32[512,256]{1,0:T(8,128)S(1)} collective-permute-done((f32[512,256]{1,0:T(8,128)S(1)}, f32[512,256]{1,0:T(8,128)S(1)}, u32[]{:S(2)}, u32[]{:S(2)}) %collective-permute-start.13) | collective-permute-done | bytes 524320 | tf_op jit(solution)/shard_map/ppermute | solution.py:332
  84.1 4.4 %collective-permute-start.17 = (f32[768,256]{1,0:T(8,128)S(1)}, f32[768,256]{1,0:T(8,128)S(1)}, u32[]{:S(2)}, u32[]{:S(2)}) collective-permute-start(f32[768,256]{1,0:T(8,128)S(1)} %get-tuple-element.209.sent), channel_id=1, source_target_pairs={{1,2},{3,4},{5,6},{7,8},{9,10},{11,12},{13,14},{15,16},{17,18},{19... | collective-permute-start | bytes 2359304 | tf_op jit(solution)/shard_map/ppermute | solution.py:323
  92.1 6.0 %collective-permute-done.17.far = f32[768,256]{1,0:T(8,128)S(1)} collective-permute-done((f32[768,256]{1,0:T(8,128)S(1)}, f32[768,256]{1,0:T(8,128)S(1)}, u32[]{:S(2)}, u32[]{:S(2)}) %collective-permute-start.17) | collective-permute-done | bytes 786464 | tf_op jit(solution)/shard_map/ppermute | solution.py:323
  99.5 3.6 %collective-permute-start.20 = (f32[768,256]{1,0:T(8,128)S(1)}, f32[768,256]{1,0:T(8,128)S(1)}, u32[]{:S(2)}, u32[]{:S(2)}) collective-permute-start(f32[768,256]{1,0:T(8,128)S(1)} %get-tuple-element.225.sent), channel_id=1, source_target_pairs={{1,2},{3,4},{5,6},{7,8},{9,10},{11,12},{13,14},{15,16},{17,18},{19... | collective-permute-start | bytes 2359304 | tf_op jit(solution)/shard_map/ppermute | solution.py:323
  106.7 6.0 %collective-permute-done.20.far = f32[768,256]{1,0:T(8,128)S(1)} collective-permute-done((f32[768,256]{1,0:T(8,128)S(1)}, f32[768,256]{1,0:T(8,128)S(1)}, u32[]{:S(2)}, u32[]{:S(2)}) %collective-permute-start.20) | collective-permute-done | bytes 786464 | tf_op jit(solution)/shard_map/ppermute | solution.py:323
  114.1 3.6 %collective-permute-start.23 = (f32[768,256]{1,0:T(8,128)S(1)}, f32[768,256]{1,0:T(8,128)S(1)}, u32[]{:S(2)}, u32[]{:S(2)}) collective-permute-start(f32[768,256]{1,0:T(8,128)S(1)} %get-tuple-element.239.sent), channel_id=1, source_target_pairs={{1,2},{3,4},{5,6},{7,8},{9,10},{11,12},{13,14},{15,16},{17,18},{19... | collective-permute-start | bytes 2359304 | tf_op jit(solution)/shard_map/ppermute | solution.py:323
  121.4 6.0 %collective-permute-done.23.far = f32[768,256]{1,0:T(8,128)S(1)} collective-permute-done((f32[768,256]{1,0:T(8,128)S(1)}, f32[768,256]{1,0:T(8,128)S(1)}, u32[]{:S(2)}, u32[]{:S(2)}) %collective-permute-start.23) | collective-permute-done | bytes 786464 | tf_op jit(solution)/shard_map/ppermute | solution.py:323
  128.8 3.6 %collective-permute-start.26 = (f32[768,256]{1,0:T(8,128)S(1)}, f32[768,256]{1,0:T(8,128)S(1)}, u32[]{:S(2)}, u32[]{:S(2)}) collective-permute-start(f32[768,256]{1,0:T(8,128)S(1)} %get-tuple-element.253.sent), channel_id=1, source_target_pairs={{1,2},{3,4},{5,6},{7,8},{9,10},{11,12},{13,14},{15,16},{17,18},{19... | collective-permute-start | bytes 2359304 | tf_op jit(solution)/shard_map/ppermute | solution.py:323
  136.6 5.5 %collective-permute-done.26.far = f32[768,256]{1,0:T(8,128)S(1)} collective-permute-done((f32[768,256]{1,0:T(8,128)S(1)}, f32[768,256]{1,0:T(8,128)S(1)}, u32[]{:S(2)}, u32[]{:S(2)}) %collective-permute-start.26) | collective-permute-done | bytes 786464 | tf_op jit(solution)/shard_map/ppermute | solution.py:323
  142.1 1.8 shard_map.229
  143.9 1.9 collective-permute-done.27.b
  145.9 36.2 %all_to_all.10.parts = f32[32,16,256]{2,1,0:T(8,128)S(1)} all-to-all(f32[32,16,256]{2,1,0:T(8,128)S(1)} %bitcast.22), channel_id=1, replica_groups={{0,2,4,6,8,10,12,14,16,18,20,22,24,26,28,30,32,34,36,38,40,42,44,46,48,..., dimensions={0} | all-to-all | bytes 1048576 | tf_op jit(solution)/shard_map/all_to_all | solution.py:415
  182.2 22.0 %all_to_all.11 = f32[32,16,256]{2,1,0:T(8,128)S(1)} all-to-all(f32[32,16,256]{2,1,0:T(8,128)S(1)} %shard_map.231), channel_id=1, replica_groups={{0,2,4,6,8,10,12,14,16,18,20,22,24,26,28,30,32,34,36,38,40,42,44,46,48,..., dimensions={0} | all-to-all | bytes 1048576 | tf_op jit(solution)/shard_map/all_to_all | solution.py:415
  204.2 4.0 %collective-permute-start.28 = (f32[512,256]{1,0:T(8,128)S(1)}, f32[512,256]{1,0:T(8,128)S(1)}, u32[]{:S(2)}, u32[]{:S(2)}) collective-permute-start(f32[512,256]{1,0:T(8,128)S(1)} %bitcast.23), channel_id=1, source_target_pairs={{0,1},{1,0},{2,3},{3,2},{4,5},{5,4},{6,7},{7,6},{8,9},{9,8},{10,11... | collective-permute-start | bytes 1572872 | tf_op jit(solution)/shard_map/ppermute | solution.py:326
  (100 shorter events, 47.6 us)
Async XLA Ops:
  6.2 14.6 %collective-permute-start.2 = (f32[768,256]{1,0:T(8,128)S(1)}, f32[768,256]{1,0:T(8,128)S(1)}, u32[]{:S(2)}, u32[]{:S(2)}) collective-permute-start(f32[768,256]{1,0:T(8,128)S(1)} %shard_map.196.sent), channel_id=1, source_target_pairs={{1,2},{3,4},{5,6},{7,8},{9,10},{11,12},{13,14},{15,16},{17,18},{19... | collective-permute-start | bytes 2359304 | tf_op jit(solution)/shard_map/ppermute | solution.py:323
  11.9 2.4 %collective-permute-start = (f32[512,256]{1,0:T(8,128)S(1)}, f32[512,256]{1,0:T(8,128)S(1)}, u32[]{:S(2)}, u32[]{:S(2)}) collective-permute-start(f32[512,256]{1,0:T(8,128)S(1)} %get-tuple-element.153), channel_id=1, source_target_pairs={{0,1},{1,0},{2,3},{3,2},{4,5},{5,4},{6,7},{7,6},{8,9},{9,8},{10,11... | collective-permute-start | bytes 1572872 | tf_op jit(solution)/shard_map/ppermute | solution.py:326
  12.0 2.3 %collective-permute-start.1 = (f32[256,256]{1,0:T(8,128)S(1)}, f32[256,256]{1,0:T(8,128)S(1)}, u32[]{:S(2)}, u32[]{:S(2)}) collective-permute-start(f32[256,256]{1,0:T(8,128)S(1)} %get-tuple-element.154), channel_id=1, source_target_pairs={{0,1},{1,0},{2,3},{3,2},{4,5},{5,4},{6,7},{7,6},{8,9},{9,8},{10,11... | collective-permute-start | bytes 786440 | tf_op jit(solution)/shard_map/ppermute | solution.py:326
  22.2 13.3 %collective-permute-start.5 = (f32[768,256]{1,0:T(8,128)S(1)}, f32[768,256]{1,0:T(8,128)S(1)}, u32[]{:S(2)}, u32[]{:S(2)}) collective-permute-start(f32[768,256]{1,0:T(8,128)S(1)} %get-tuple-element.163.sent), channel_id=1, source_target_pairs={{1,2},{3,4},{5,6},{7,8},{9,10},{11,12},{13,14},{15,16},{17,18},{19... | collective-permute-start | bytes 2359304 | tf_op jit(solution)/shard_map/ppermute | solution.py:323
  26.6 2.4 %collective-permute-start.3 = (f32[512,256]{1,0:T(8,128)S(1)}, f32[512,256]{1,0:T(8,128)S(1)}, u32[]{:S(2)}, u32[]{:S(2)}) collective-permute-start(f32[512,256]{1,0:T(8,128)S(1)} %get-tuple-element.168), channel_id=1, source_target_pairs={{0,1},{1,0},{2,3},{3,2},{4,5},{5,4},{6,7},{7,6},{8,9},{9,8},{10,11... | collective-permute-start | bytes 1572872 | tf_op jit(solution)/shard_map/ppermute | solution.py:326
  26.7 2.3 %collective-permute-start.4 = (f32[256,256]{1,0:T(8,128)S(1)}, f32[256,256]{1,0:T(8,128)S(1)}, u32[]{:S(2)}, u32[]{:S(2)}) collective-permute-start(f32[256,256]{1,0:T(8,128)S(1)} %get-tuple-element.169), channel_id=1, source_target_pairs={{0,1},{1,0},{2,3},{3,2},{4,5},{5,4},{6,7},{7,6},{8,9},{9,8},{10,11... | collective-permute-start | bytes 786440 | tf_op jit(solution)/shard_map/ppermute | solution.py:326
  36.8 13.3 %collective-permute-start.8 = (f32[768,256]{1,0:T(8,128)S(1)}, f32[768,256]{1,0:T(8,128)S(1)}, u32[]{:S(2)}, u32[]{:S(2)}) collective-permute-start(f32[768,256]{1,0:T(8,128)S(1)} %get-tuple-element.176.sent), channel_id=1, source_target_pairs={{1,2},{3,4},{5,6},{7,8},{9,10},{11,12},{13,14},{15,16},{17,18},{19... | collective-permute-start | bytes 2359304 | tf_op jit(solution)/shard_map/ppermute | solution.py:323
  41.2 2.4 %collective-permute-start.6 = (f32[512,256]{1,0:T(8,128)S(1)}, f32[512,256]{1,0:T(8,128)S(1)}, u32[]{:S(2)}, u32[]{:S(2)}) collective-permute-start(f32[512,256]{1,0:T(8,128)S(1)} %get-tuple-element.182), channel_id=1, source_target_pairs={{0,1},{1,0},{2,3},{3,2},{4,5},{5,4},{6,7},{7,6},{8,9},{9,8},{10,11... | collective-permute-start | bytes 1572872 | tf_op jit(solution)/shard_map/ppermute | solution.py:326
  51.5 13.6 %collective-permute-start.11 = (f32[768,256]{1,0:T(8,128)S(1)}, f32[768,256]{1,0:T(8,128)S(1)}, u32[]{:S(2)}, u32[]{:S(2)}) collective-permute-start(f32[768,256]{1,0:T(8,128)S(1)} %get-tuple-element.190.sent), channel_id=1, source_target_pairs={{1,2},{3,4},{5,6},{7,8},{9,10},{11,12},{13,14},{15,16},{17,18},{19... | collective-permute-start | bytes 2359304 | tf_op jit(solution)/shard_map/ppermute | solution.py:323
  56.0 2.4 %collective-permute-start.9 = (f32[512,256]{1,0:T(8,128)S(1)}, f32[512,256]{1,0:T(8,128)S(1)}, u32[]{:S(2)}, u32[]{:S(2)}) collective-permute-start(f32[512,256]{1,0:T(8,128)S(1)} %get-tuple-element.196), channel_id=1, source_target_pairs={{0,1},{1,0},{2,3},{3,2},{4,5},{5,4},{6,7},{7,6},{8,9},{9,8},{10,11... | collective-permute-start | bytes 1572872 | tf_op jit(solution)/shard_map/ppermute | solution.py:326
  56.1 2.3 %collective-permute-start.10 = (f32[256,256]{1,0:T(8,128)S(1)}, f32[256,256]{1,0:T(8,128)S(1)}, u32[]{:S(2)}, u32[]{:S(2)}) collective-permute-start(f32[256,256]{1,0:T(8,128)S(1)} %get-tuple-element.197), channel_id=1, source_target_pairs={{0,1},{1,0},{2,3},{3,2},{4,5},{5,4},{6,7},{7,6},{8,9},{9,8},{10,11... | collective-permute-start | bytes 786440 | tf_op jit(solution)/shard_map/ppermute | solution.py:326
  56.6 15.5 %collective-permute-start.12 = (f32[512,256]{1,0:T(8,128)S(1)}, f32[512,256]{1,0:T(8,128)S(1)}, u32[]{:S(2)}, u32[]{:S(2)}) collective-permute-start(f32[512,256]{1,0:T(8,128)S(1)} %get-tuple-element.206), channel_id=1, source_target_pairs={{64,0},{128,64},{192,128},{65,1},{129,65},{193,129},{66,2},{130,66... | collective-permute-start | bytes 1572872 | tf_op jit(solution)/shard_map/ppermute | solution.py:332
  66.8 16.5 %collective-permute-start.13 = (f32[512,256]{1,0:T(8,128)S(1)}, f32[512,256]{1,0:T(8,128)S(1)}, u32[]{:S(2)}, u32[]{:S(2)}) collective-permute-start(f32[512,256]{1,0:T(8,128)S(1)} %get-tuple-element.207), channel_id=1, source_target_pairs={{64,0},{128,64},{192,128},{65,1},{129,65},{193,129},{66,2},{130,66... | collective-permute-start | bytes 1572872 | tf_op jit(solution)/shard_map/ppermute | solution.py:332
  68.1 15.2 %collective-permute-start.14 = (f32[512,256]{1,0:T(8,128)S(1)}, f32[512,256]{1,0:T(8,128)S(1)}, u32[]{:S(2)}, u32[]{:S(2)}) collective-permute-start(f32[512,256]{1,0:T(8,128)S(1)} %get-tuple-element.208), channel_id=1, source_target_pairs={{0,64},{64,128},{128,192},{1,65},{65,129},{129,193},{2,66},{66,130... | collective-permute-start | bytes 1572872 | tf_op jit(solution)/shard_map/ppermute | solution.py:329
  84.1 14.0 %collective-permute-start.17 = (f32[768,256]{1,0:T(8,128)S(1)}, f32[768,256]{1,0:T(8,128)S(1)}, u32[]{:S(2)}, u32[]{:S(2)}) collective-permute-start(f32[768,256]{1,0:T(8,128)S(1)} %get-tuple-element.209.sent), channel_id=1, source_target_pairs={{1,2},{3,4},{5,6},{7,8},{9,10},{11,12},{13,14},{15,16},{17,18},{19... | collective-permute-start | bytes 2359304 | tf_op jit(solution)/shard_map/ppermute | solution.py:323
  89.2 2.4 %collective-permute-start.15 = (f32[512,256]{1,0:T(8,128)S(1)}, f32[512,256]{1,0:T(8,128)S(1)}, u32[]{:S(2)}, u32[]{:S(2)}) collective-permute-start(f32[512,256]{1,0:T(8,128)S(1)} %get-tuple-element.216), channel_id=1, source_target_pairs={{0,1},{1,0},{2,3},{3,2},{4,5},{5,4},{6,7},{7,6},{8,9},{9,8},{10,11... | collective-permute-start | bytes 1572872 | tf_op jit(solution)/shard_map/ppermute | solution.py:326
  99.5 13.3 %collective-permute-start.20 = (f32[768,256]{1,0:T(8,128)S(1)}, f32[768,256]{1,0:T(8,128)S(1)}, u32[]{:S(2)}, u32[]{:S(2)}) collective-permute-start(f32[768,256]{1,0:T(8,128)S(1)} %get-tuple-element.225.sent), channel_id=1, source_target_pairs={{1,2},{3,4},{5,6},{7,8},{9,10},{11,12},{13,14},{15,16},{17,18},{19... | collective-permute-start | bytes 2359304 | tf_op jit(solution)/shard_map/ppermute | solution.py:323
  103.8 2.4 %collective-permute-start.18 = (f32[512,256]{1,0:T(8,128)S(1)}, f32[512,256]{1,0:T(8,128)S(1)}, u32[]{:S(2)}, u32[]{:S(2)}) collective-permute-start(f32[512,256]{1,0:T(8,128)S(1)} %get-tuple-element.231), channel_id=1, source_target_pairs={{0,1},{1,0},{2,3},{3,2},{4,5},{5,4},{6,7},{7,6},{8,9},{9,8},{10,11... | collective-permute-start | bytes 1572872 | tf_op jit(solution)/shard_map/ppermute | solution.py:326
  114.1 13.3 %collective-permute-start.23 = (f32[768,256]{1,0:T(8,128)S(1)}, f32[768,256]{1,0:T(8,128)S(1)}, u32[]{:S(2)}, u32[]{:S(2)}) collective-permute-start(f32[768,256]{1,0:T(8,128)S(1)} %get-tuple-element.239.sent), channel_id=1, source_target_pairs={{1,2},{3,4},{5,6},{7,8},{9,10},{11,12},{13,14},{15,16},{17,18},{19... | collective-permute-start | bytes 2359304 | tf_op jit(solution)/shard_map/ppermute | solution.py:323
  118.5 2.4 %collective-permute-start.21 = (f32[512,256]{1,0:T(8,128)S(1)}, f32[512,256]{1,0:T(8,128)S(1)}, u32[]{:S(2)}, u32[]{:S(2)}) collective-permute-start(f32[512,256]{1,0:T(8,128)S(1)} %get-tuple-element.245), channel_id=1, source_target_pairs={{0,1},{1,0},{2,3},{3,2},{4,5},{5,4},{6,7},{7,6},{8,9},{9,8},{10,11... | collective-permute-start | bytes 1572872 | tf_op jit(solution)/shard_map/ppermute | solution.py:326
  128.8 13.3 %collective-permute-start.26 = (f32[768,256]{1,0:T(8,128)S(1)}, f32[768,256]{1,0:T(8,128)S(1)}, u32[]{:S(2)}, u32[]{:S(2)}) collective-permute-start(f32[768,256]{1,0:T(8,128)S(1)} %get-tuple-element.253.sent), channel_id=1, source_target_pairs={{1,2},{3,4},{5,6},{7,8},{9,10},{11,12},{13,14},{15,16},{17,18},{19... | collective-permute-start | bytes 2359304 | tf_op jit(solution)/shard_map/ppermute | solution.py:323
  133.1 2.9 %collective-permute-start.24 = (f32[512,256]{1,0:T(8,128)S(1)}, f32[512,256]{1,0:T(8,128)S(1)}, u32[]{:S(2)}, u32[]{:S(2)}) collective-permute-start(f32[512,256]{1,0:T(8,128)S(1)} %get-tuple-element.259), channel_id=1, source_target_pairs={{0,1},{1,0},{2,3},{3,2},{4,5},{5,4},{6,7},{7,6},{8,9},{9,8},{10,11... | collective-permute-start | bytes 1572872 | tf_op jit(solution)/shard_map/ppermute | solution.py:326
  133.2 2.8 %collective-permute-start.25 = (f32[256,256]{1,0:T(8,128)S(1)}, f32[256,256]{1,0:T(8,128)S(1)}, u32[]{:S(2)}, u32[]{:S(2)}) collective-permute-start(f32[256,256]{1,0:T(8,128)S(1)} %get-tuple-element.260), channel_id=1, source_target_pairs={{0,1},{1,0},{2,3},{3,2},{4,5},{5,4},{6,7},{7,6},{8,9},{9,8},{10,11... | collective-permute-start | bytes 786440 | tf_op jit(solution)/shard_map/ppermute | solution.py:326
  204.2 5.6 %collective-permute-start.28 = (f32[512,256]{1,0:T(8,128)S(1)}, f32[512,256]{1,0:T(8,128)S(1)}, u32[]{:S(2)}, u32[]{:S(2)}) collective-permute-start(f32[512,256]{1,0:T(8,128)S(1)} %bitcast.23), channel_id=1, source_target_pairs={{0,1},{1,0},{2,3},{3,2},{4,5},{5,4},{6,7},{7,6},{8,9},{9,8},{10,11... | collective-permute-start | bytes 1572872 | tf_op jit(solution)/shard_map/ppermute | solution.py:326
  (18 other events, 91.4 us)
where the time goes:
time: 211 us
  waiting for transfers between devices  73.2 us (35%)
  blocking collectives  58.2 us (28%)
  starting transfers between devices  46.6 us (22%)
  Pallas kernels  28.1 us (13%)
  local copies, waits for them, and re-layouts  3.48 us (2%)
    all_to_all x2, blocking collectives, exchanged(): return lax.all_to_all(v, 'dom', 0, 0, axis_index_groups=groups, tiled=True)  58.2 us
    ppermute x8, waiting for transfers between devices, far(): return lax.ppermute(v, 'dom', far_pairs)  47.9 us
    ppermute x8, starting transfers between devices, far(): return lax.ppermute(v, 'dom', far_pairs)  31.3 us
    pallas_call x38, Pallas kernels, run(): pl.pallas_call(kernel, out_shape=[jax.ShapeDtypeStruct(s, t) for s, t in...  28.1 us
    ppermute x18, waiting for transfers between devices, near(): return lax.ppermute(v, 'dom', sib_pairs)  14.2 us
    ppermute x2, waiting for transfers between devices, backward(): return lax.ppermute(v, 'segment', [(i + 1, i) for i in range(last)])  11.1 us
    ppermute x18, starting transfers between devices, near(): return lax.ppermute(v, 'dom', sib_pairs)  8.75 us
  transfers between devices with their start and end apart: 29, of which 18 were waited for; matrix products, arithmetic and copies ran while one was open for 0% of the time, Pallas kernels for 7%

commit v1 on v0

--- a/solution.py
+++ b/solution.py
@@ -35,12 +35,15 @@
 
 
 def dot3(a, b):
-    return mm(a[0], b[0]) + (mm(a[0], b[1]) + mm(a[1], b[0]))
+    return mm(jnp.concatenate([a[0], a[0], a[1]], axis=1), jnp.concatenate([b[0], b[1], b[0]], axis=0))
 
 
 def dot6(a, b):
-    small = mm(a[0], b[2]) + (mm(a[2], b[0]) + mm(a[1], b[1]))
-    return mm(a[0], b[0]) + ((mm(a[0], b[1]) + mm(a[1], b[0])) + small)
+    n = a[0].shape[0]
+    p = mm(jnp.concatenate([a[0], a[1], a[2]], axis=0), b[0])
+    q = mm(jnp.concatenate([a[0], a[1]], axis=0), b[1])
+    small = mm(a[0], b[2]) + (p[2 * n :] + q[n:])
+    return p[:n] + ((q[:n] + p[n : 2 * n]) + small)
 
 
 def norm(h):
@@ -242,13 +245,21 @@
     refs[-1][...] = value + refs[0][...] if len(refs) > 1 else value
 
 
+def final_grad_kernel(
+    k, owed, far, xhat, gains, before, first_high, second_low, second_high, keep, give
+):
+    grad = before[...] + weight_grad(k, xhat[...], owed[...] + far[B, :], gains)
+    even = lax.rem(lax.axis_index("dom"), 2) == 0
+    keep[A, :] = jnp.where(even, grad, second_low[...])
+    keep[B, :] = jnp.where(even, first_high[...], second_high[...])
+    give[A, :] = jnp.where(even, second_low[...], grad)
+    give[B, :] = jnp.where(even, second_high[...], first_high[...])
+
+
 def last_kernel(
     final, k, inverse, owed, forward, far, xhat, rstd, cot, band, gains, turned, low, top_cot, top,
-    *refs,
-):
-    if final:
-        before, first_high, second_low, second_high, *refs = refs
-    whole, whole_cot, whole_ahead, *refs = refs
+    whole, whole_cot, whole_ahead, *refs,
+):
     value, back, carried, ahead = joined(
         k, inverse, owed, forward, far, xhat, rstd, cot, band, gains, turned
     )
@@ -258,15 +269,7 @@
     whole_cot[:, B] = carried
     whole_ahead[:, A] = top[...]
     whole_ahead[:, B] = ahead
-    if final:
-        keep, give = refs
-        grad = before[...] + weight_grad(k, xhat[...], back, gains)
-        even = lax.rem(lax.axis_index("dom"), 2) == 0
-        keep[A, :] = jnp.where(even, grad, second_low[...])
-        keep[B, :] = jnp.where(even, first_high[...], second_high[...])
-        give[A, :] = jnp.where(even, second_low[...], grad)
-        give[B, :] = jnp.where(even, second_high[...], first_high[...])
-    else:
+    if not final:
         back_out, late, ahead_out = refs
         back_out[...] = back
         late[A, :] = value
@@ -391,10 +394,14 @@
                 )
                 late, onwards = backward(late), onward(onwards)
             else:
-                *wholes, keep, give = run(
-                    part(last_kernel, True, k), [FULL, FULL, FULL, PAIR, PAIR], *operands, y2, g1,
-                    x1, grads[at(FIRST, 0)], grads[at(FIRST, 1)], grads[at(SECOND, 0)],
-                    grads[at(SECOND, 1)], flops=5 * PRODUCT,
+                keep, give = run(
+                    part(final_grad_kernel, k), [PAIR, PAIR], owed, from_far, xhat, gains,
+                    grads[at(FIRST, 0)], grads[at(FIRST, 1)], grads[at(SECOND, 0)],
+                    grads[at(SECOND, 1)], flops=PRODUCT,
+                )
+                wholes = run(
+                    part(last_kernel, True, k), [FULL, FULL, FULL], *operands, y2, g1, x1,
+                    flops=5 * PRODUCT,
                 )
                 break
             before = [grads[k]] if k in grads else []

time: 211 us -> 210 us (level)
    pallas_call x38 -> x39, Pallas kernels: 28.1 us -> 28.3 us  [run(): pl.pallas_call(kernel, out_shape=[jax.ShapeDtypeStruct(s, t) for s, t in...]
  transfers between devices with their start and end apart: 29 -> 29, of which waited for: 18 -> 17; matrix products, arithmetic and copies ran while one was open for 0% -> 0% of each run, Pallas kernels for 7% -> 8%
where the time goes in v1:
time: 210 us
  waiting for transfers between devices  71.7 us (34%)
  blocking collectives  58.2 us (28%)
  starting transfers between devices  46.8 us (22%)
  Pallas kernels  28.3 us (13%)
  local copies, waits for them, and re-layouts  3.48 us (2%)
    all_to_all x2, blocking collectives, exchanged(): return lax.all_to_all(v, 'dom', 0, 0, axis_index_groups=groups, tiled=True)  58.2 us
    ppermute x8, waiting for transfers between devices, far(): return lax.ppermute(v, 'dom', far_pairs)  47.9 us
    ppermute x8, starting transfers between devices, far(): return lax.ppermute(v, 'dom', far_pairs)  31.3 us
    pallas_call x39, Pallas kernels, run(): pl.pallas_call(kernel, out_shape=[jax.ShapeDtypeStruct(s, t) for s, t in...  28.3 us
    ppermute x18, waiting for transfers between devices, near(): return lax.ppermute(v, 'dom', sib_pairs)  12.7 us
    ppermute x2, waiting for transfers between devices, backward(): return lax.ppermute(v, 'segment', [(i + 1, i) for i in range(last)])  11.1 us
    ppermute x18, starting transfers between devices, near(): return lax.ppermute(v, 'dom', sib_pairs)  8.84 us
  transfers between devices with their start and end apart: 29, of which 17 were waited for; matrix products, arithmetic and copies ran while one was open for 0% of the time, Pallas kernels for 8%

profile of v1, /device:TPU:1, one launch (start us, length us, event | category | flops | bytes accessed | tf_op | source)
XLA Modules:
  0.0 209.7 jit_solution(3491795947017056740)
XLA Ops:
  6.2 4.9 %collective-permute-start.2 = (f32[768,256]{1,0:T(8,128)S(1)}, f32[768,256]{1,0:T(8,128)S(1)}, u32[]{:S(2)}, u32[]{:S(2)}) collective-permute-start(f32[768,256]{1,0:T(8,128)S(1)} %shard_map.196.sent), channel_id=1, source_target_pairs={{1,2},{3,4},{5,6},{7,8},{9,10},{11,12},{13,14},{15,16},{17,18},{19... | collective-permute-start | bytes 2359304 | tf_op jit(solution)/shard_map/ppermute | solution.py:326
  14.8 6.1 %collective-permute-done.2.far = f32[768,256]{1,0:T(8,128)S(1)} collective-permute-done((f32[768,256]{1,0:T(8,128)S(1)}, f32[768,256]{1,0:T(8,128)S(1)}, u32[]{:S(2)}, u32[]{:S(2)}) %collective-permute-start.2) | collective-permute-done | bytes 786464 | tf_op jit(solution)/shard_map/ppermute | solution.py:326
  22.2 3.6 %collective-permute-start.5 = (f32[768,256]{1,0:T(8,128)S(1)}, f32[768,256]{1,0:T(8,128)S(1)}, u32[]{:S(2)}, u32[]{:S(2)}) collective-permute-start(f32[768,256]{1,0:T(8,128)S(1)} %get-tuple-element.163.sent), channel_id=1, source_target_pairs={{1,2},{3,4},{5,6},{7,8},{9,10},{11,12},{13,14},{15,16},{17,18},{19... | collective-permute-start | bytes 2359304 | tf_op jit(solution)/shard_map/ppermute | solution.py:326
  27.1 1.8 collective-permute-done.4.near_owed
  29.5 6.0 %collective-permute-done.5.far = f32[768,256]{1,0:T(8,128)S(1)} collective-permute-done((f32[768,256]{1,0:T(8,128)S(1)}, f32[768,256]{1,0:T(8,128)S(1)}, u32[]{:S(2)}, u32[]{:S(2)}) %collective-permute-start.5) | collective-permute-done | bytes 786464 | tf_op jit(solution)/shard_map/ppermute | solution.py:326
  36.8 3.6 %collective-permute-start.8 = (f32[768,256]{1,0:T(8,128)S(1)}, f32[768,256]{1,0:T(8,128)S(1)}, u32[]{:S(2)}, u32[]{:S(2)}) collective-permute-start(f32[768,256]{1,0:T(8,128)S(1)} %get-tuple-element.176.sent), channel_id=1, source_target_pairs={{1,2},{3,4},{5,6},{7,8},{9,10},{11,12},{13,14},{15,16},{17,18},{19... | collective-permute-start | bytes 2359304 | tf_op jit(solution)/shard_map/ppermute | solution.py:326
  44.1 6.0 %collective-permute-done.8.far = f32[768,256]{1,0:T(8,128)S(1)} collective-permute-done((f32[768,256]{1,0:T(8,128)S(1)}, f32[768,256]{1,0:T(8,128)S(1)}, u32[]{:S(2)}, u32[]{:S(2)}) %collective-permute-start.8) | collective-permute-done | bytes 786464 | tf_op jit(solution)/shard_map/ppermute | solution.py:326
  51.5 3.8 %collective-permute-start.11 = (f32[768,256]{1,0:T(8,128)S(1)}, f32[768,256]{1,0:T(8,128)S(1)}, u32[]{:S(2)}, u32[]{:S(2)}) collective-permute-start(f32[768,256]{1,0:T(8,128)S(1)} %get-tuple-element.190.sent), channel_id=1, source_target_pairs={{1,2},{3,4},{5,6},{7,8},{9,10},{11,12},{13,14},{15,16},{17,18},{19... | collective-permute-start | bytes 2359304 | tf_op jit(solution)/shard_map/ppermute | solution.py:326
  59.0 6.2 %collective-permute-done.11.far = f32[768,256]{1,0:T(8,128)S(1)} collective-permute-done((f32[768,256]{1,0:T(8,128)S(1)}, f32[768,256]{1,0:T(8,128)S(1)}, u32[]{:S(2)}, u32[]{:S(2)}) %collective-permute-start.11) | collective-permute-done | bytes 786464 | tf_op jit(solution)/shard_map/ppermute | solution.py:326
  68.1 4.0 %collective-permute-start.14 = (f32[512,256]{1,0:T(8,128)S(1)}, f32[512,256]{1,0:T(8,128)S(1)}, u32[]{:S(2)}, u32[]{:S(2)}) collective-permute-start(f32[512,256]{1,0:T(8,128)S(1)} %get-tuple-element.208), channel_id=1, source_target_pairs={{0,64},{64,128},{128,192},{1,65},{65,129},{129,193},{2,66},{66,130... | collective-permute-start | bytes 1572872 | tf_op jit(solution)/shard_map/ppermute | solution.py:332
  72.2 11.1 %collective-permute-done.13.late = f32[512,256]{1,0:T(8,128)S(1)} collective-permute-done((f32[512,256]{1,0:T(8,128)S(1)}, f32[512,256]{1,0:T(8,128)S(1)}, u32[]{:S(2)}, u32[]{:S(2)}) %collective-permute-start.13) | collective-permute-done | bytes 524320 | tf_op jit(solution)/shard_map/ppermute | solution.py:335
  84.1 4.4 %collective-permute-start.17 = (f32[768,256]{1,0:T(8,128)S(1)}, f32[768,256]{1,0:T(8,128)S(1)}, u32[]{:S(2)}, u32[]{:S(2)}) collective-permute-start(f32[768,256]{1,0:T(8,128)S(1)} %get-tuple-element.209.sent), channel_id=1, source_target_pairs={{1,2},{3,4},{5,6},{7,8},{9,10},{11,12},{13,14},{15,16},{17,18},{19... | collective-permute-start | bytes 2359304 | tf_op jit(solution)/shard_map/ppermute | solution.py:326
  89.8 1.8 collective-permute-done.16.near_owed
  92.1 6.0 %collective-permute-done.17.far = f32[768,256]{1,0:T(8,128)S(1)} collective-permute-done((f32[768,256]{1,0:T(8,128)S(1)}, f32[768,256]{1,0:T(8,128)S(1)}, u32[]{:S(2)}, u32[]{:S(2)}) %collective-permute-start.17) | collective-permute-done | bytes 786464 | tf_op jit(solution)/shard_map/ppermute | solution.py:326
  99.5 3.6 %collective-permute-start.20 = (f32[768,256]{1,0:T(8,128)S(1)}, f32[768,256]{1,0:T(8,128)S(1)}, u32[]{:S(2)}, u32[]{:S(2)}) collective-permute-start(f32[768,256]{1,0:T(8,128)S(1)} %get-tuple-element.225.sent), channel_id=1, source_target_pairs={{1,2},{3,4},{5,6},{7,8},{9,10},{11,12},{13,14},{15,16},{17,18},{19... | collective-permute-start | bytes 2359304 | tf_op jit(solution)/shard_map/ppermute | solution.py:326
  106.8 6.0 %collective-permute-done.20.far = f32[768,256]{1,0:T(8,128)S(1)} collective-permute-done((f32[768,256]{1,0:T(8,128)S(1)}, f32[768,256]{1,0:T(8,128)S(1)}, u32[]{:S(2)}, u32[]{:S(2)}) %collective-permute-start.20) | collective-permute-done | bytes 786464 | tf_op jit(solution)/shard_map/ppermute | solution.py:326
  114.2 3.6 %collective-permute-start.23 = (f32[768,256]{1,0:T(8,128)S(1)}, f32[768,256]{1,0:T(8,128)S(1)}, u32[]{:S(2)}, u32[]{:S(2)}) collective-permute-start(f32[768,256]{1,0:T(8,128)S(1)} %get-tuple-element.239.sent), channel_id=1, source_target_pairs={{1,2},{3,4},{5,6},{7,8},{9,10},{11,12},{13,14},{15,16},{17,18},{19... | collective-permute-start | bytes 2359304 | tf_op jit(solution)/shard_map/ppermute | solution.py:326
  121.5 6.0 %collective-permute-done.23.far = f32[768,256]{1,0:T(8,128)S(1)} collective-permute-done((f32[768,256]{1,0:T(8,128)S(1)}, f32[768,256]{1,0:T(8,128)S(1)}, u32[]{:S(2)}, u32[]{:S(2)}) %collective-permute-start.23) | collective-permute-done | bytes 786464 | tf_op jit(solution)/shard_map/ppermute | solution.py:326
  128.8 3.6 %collective-permute-start.26 = (f32[768,256]{1,0:T(8,128)S(1)}, f32[768,256]{1,0:T(8,128)S(1)}, u32[]{:S(2)}, u32[]{:S(2)}) collective-permute-start(f32[768,256]{1,0:T(8,128)S(1)} %get-tuple-element.253.sent), channel_id=1, source_target_pairs={{1,2},{3,4},{5,6},{7,8},{9,10},{11,12},{13,14},{15,16},{17,18},{19... | collective-permute-start | bytes 2359304 | tf_op jit(solution)/shard_map/ppermute | solution.py:326
  136.6 5.5 %collective-permute-done.26.far = f32[768,256]{1,0:T(8,128)S(1)} collective-permute-done((f32[768,256]{1,0:T(8,128)S(1)}, f32[768,256]{1,0:T(8,128)S(1)}, u32[]{:S(2)}, u32[]{:S(2)}) %collective-permute-start.26) | collective-permute-done | bytes 786464 | tf_op jit(solution)/shard_map/ppermute | solution.py:326
  142.6 1.9 collective-permute-done.27.b
  144.6 36.2 %all_to_all.10.parts = f32[32,16,256]{2,1,0:T(8,128)S(1)} all-to-all(f32[32,16,256]{2,1,0:T(8,128)S(1)} %bitcast.22), channel_id=1, replica_groups={{0,2,4,6,8,10,12,14,16,18,20,22,24,26,28,30,32,34,36,38,40,42,44,46,48,..., dimensions={0} | all-to-all | bytes 1048576 | tf_op jit(solution)/shard_map/all_to_all | solution.py:422
  180.9 22.0 %all_to_all.11 = f32[32,16,256]{2,1,0:T(8,128)S(1)} all-to-all(f32[32,16,256]{2,1,0:T(8,128)S(1)} %shard_map.232), channel_id=1, replica_groups={{0,2,4,6,8,10,12,14,16,18,20,22,24,26,28,30,32,34,36,38,40,42,44,46,48,..., dimensions={0} | all-to-all | bytes 1048576 | tf_op jit(solution)/shard_map/all_to_all | solution.py:422
  202.8 4.0 %collective-permute-start.28 = (f32[512,256]{1,0:T(8,128)S(1)}, f32[512,256]{1,0:T(8,128)S(1)}, u32[]{:S(2)}, u32[]{:S(2)}) collective-permute-start(f32[512,256]{1,0:T(8,128)S(1)} %bitcast.23), channel_id=1, source_target_pairs={{0,1},{1,0},{2,3},{3,2},{4,5},{5,4},{6,7},{7,6},{8,9},{9,8},{10,11... | collective-permute-start | bytes 1572872 | tf_op jit(solution)/shard_map/ppermute | solution.py:329
  (101 shorter events, 46.5 us)
Async XLA Ops:
  6.2 14.6 %collective-permute-start.2 = (f32[768,256]{1,0:T(8,128)S(1)}, f32[768,256]{1,0:T(8,128)S(1)}, u32[]{:S(2)}, u32[]{:S(2)}) collective-permute-start(f32[768,256]{1,0:T(8,128)S(1)} %shard_map.196.sent), channel_id=1, source_target_pairs={{1,2},{3,4},{5,6},{7,8},{9,10},{11,12},{13,14},{15,16},{17,18},{19... | collective-permute-start | bytes 2359304 | tf_op jit(solution)/shard_map/ppermute | solution.py:326
  11.9 2.4 %collective-permute-start = (f32[512,256]{1,0:T(8,128)S(1)}, f32[512,256]{1,0:T(8,128)S(1)}, u32[]{:S(2)}, u32[]{:S(2)}) collective-permute-start(f32[512,256]{1,0:T(8,128)S(1)} %get-tuple-element.153), channel_id=1, source_target_pairs={{0,1},{1,0},{2,3},{3,2},{4,5},{5,4},{6,7},{7,6},{8,9},{9,8},{10,11... | collective-permute-start | bytes 1572872 | tf_op jit(solution)/shard_map/ppermute | solution.py:329
  12.0 2.3 %collective-permute-start.1 = (f32[256,256]{1,0:T(8,128)S(1)}, f32[256,256]{1,0:T(8,128)S(1)}, u32[]{:S(2)}, u32[]{:S(2)}) collective-permute-start(f32[256,256]{1,0:T(8,128)S(1)} %get-tuple-element.154), channel_id=1, source_target_pairs={{0,1},{1,0},{2,3},{3,2},{4,5},{5,4},{6,7},{7,6},{8,9},{9,8},{10,11... | collective-permute-start | bytes 786440 | tf_op jit(solution)/shard_map/ppermute | solution.py:329
  22.2 13.3 %collective-permute-start.5 = (f32[768,256]{1,0:T(8,128)S(1)}, f32[768,256]{1,0:T(8,128)S(1)}, u32[]{:S(2)}, u32[]{:S(2)}) collective-permute-start(f32[768,256]{1,0:T(8,128)S(1)} %get-tuple-element.163.sent), channel_id=1, source_target_pairs={{1,2},{3,4},{5,6},{7,8},{9,10},{11,12},{13,14},{15,16},{17,18},{19... | collective-permute-start | bytes 2359304 | tf_op jit(solution)/shard_map/ppermute | solution.py:326
  26.6 2.4 %collective-permute-start.3 = (f32[512,256]{1,0:T(8,128)S(1)}, f32[512,256]{1,0:T(8,128)S(1)}, u32[]{:S(2)}, u32[]{:S(2)}) collective-permute-start(f32[512,256]{1,0:T(8,128)S(1)} %get-tuple-element.168), channel_id=1, source_target_pairs={{0,1},{1,0},{2,3},{3,2},{4,5},{5,4},{6,7},{7,6},{8,9},{9,8},{10,11... | collective-permute-start | bytes 1572872 | tf_op jit(solution)/shard_map/ppermute | solution.py:329
  36.8 13.3 %collective-permute-start.8 = (f32[768,256]{1,0:T(8,128)S(1)}, f32[768,256]{1,0:T(8,128)S(1)}, u32[]{:S(2)}, u32[]{:S(2)}) collective-permute-start(f32[768,256]{1,0:T(8,128)S(1)} %get-tuple-element.176.sent), channel_id=1, source_target_pairs={{1,2},{3,4},{5,6},{7,8},{9,10},{11,12},{13,14},{15,16},{17,18},{19... | collective-permute-start | bytes 2359304 | tf_op jit(solution)/shard_map/ppermute | solution.py:326
  41.2 2.4 %collective-permute-start.6 = (f32[512,256]{1,0:T(8,128)S(1)}, f32[512,256]{1,0:T(8,128)S(1)}, u32[]{:S(2)}, u32[]{:S(2)}) collective-permute-start(f32[512,256]{1,0:T(8,128)S(1)} %get-tuple-element.182), channel_id=1, source_target_pairs={{0,1},{1,0},{2,3},{3,2},{4,5},{5,4},{6,7},{7,6},{8,9},{9,8},{10,11... | collective-permute-start | bytes 1572872 | tf_op jit(solution)/shard_map/ppermute | solution.py:329
  51.5 13.6 %collective-permute-start.11 = (f32[768,256]{1,0:T(8,128)S(1)}, f32[768,256]{1,0:T(8,128)S(1)}, u32[]{:S(2)}, u32[]{:S(2)}) collective-permute-start(f32[768,256]{1,0:T(8,128)S(1)} %get-tuple-element.190.sent), channel_id=1, source_target_pairs={{1,2},{3,4},{5,6},{7,8},{9,10},{11,12},{13,14},{15,16},{17,18},{19... | collective-permute-start | bytes 2359304 | tf_op jit(solution)/shard_map/ppermute | solution.py:326
  56.0 2.4 %collective-permute-start.9 = (f32[512,256]{1,0:T(8,128)S(1)}, f32[512,256]{1,0:T(8,128)S(1)}, u32[]{:S(2)}, u32[]{:S(2)}) collective-permute-start(f32[512,256]{1,0:T(8,128)S(1)} %get-tuple-element.196), channel_id=1, source_target_pairs={{0,1},{1,0},{2,3},{3,2},{4,5},{5,4},{6,7},{7,6},{8,9},{9,8},{10,11... | collective-permute-start | bytes 1572872 | tf_op jit(solution)/shard_map/ppermute | solution.py:329
  56.1 2.3 %collective-permute-start.10 = (f32[256,256]{1,0:T(8,128)S(1)}, f32[256,256]{1,0:T(8,128)S(1)}, u32[]{:S(2)}, u32[]{:S(2)}) collective-permute-start(f32[256,256]{1,0:T(8,128)S(1)} %get-tuple-element.197), channel_id=1, source_target_pairs={{0,1},{1,0},{2,3},{3,2},{4,5},{5,4},{6,7},{7,6},{8,9},{9,8},{10,11... | collective-permute-start | bytes 786440 | tf_op jit(solution)/shard_map/ppermute | solution.py:329
  56.6 15.5 %collective-permute-start.12 = (f32[512,256]{1,0:T(8,128)S(1)}, f32[512,256]{1,0:T(8,128)S(1)}, u32[]{:S(2)}, u32[]{:S(2)}) collective-permute-start(f32[512,256]{1,0:T(8,128)S(1)} %get-tuple-element.206), channel_id=1, source_target_pairs={{64,0},{128,64},{192,128},{65,1},{129,65},{193,129},{66,2},{130,66... | collective-permute-start | bytes 1572872 | tf_op jit(solution)/shard_map/ppermute | solution.py:335
  66.8 16.4 %collective-permute-start.13 = (f32[512,256]{1,0:T(8,128)S(1)}, f32[512,256]{1,0:T(8,128)S(1)}, u32[]{:S(2)}, u32[]{:S(2)}) collective-permute-start(f32[512,256]{1,0:T(8,128)S(1)} %get-tuple-element.207), channel_id=1, source_target_pairs={{64,0},{128,64},{192,128},{65,1},{129,65},{193,129},{66,2},{130,66... | collective-permute-start | bytes 1572872 | tf_op jit(solution)/shard_map/ppermute | solution.py:335
  68.1 15.1 %collective-permute-start.14 = (f32[512,256]{1,0:T(8,128)S(1)}, f32[512,256]{1,0:T(8,128)S(1)}, u32[]{:S(2)}, u32[]{:S(2)}) collective-permute-start(f32[512,256]{1,0:T(8,128)S(1)} %get-tuple-element.208), channel_id=1, source_target_pairs={{0,64},{64,128},{128,192},{1,65},{65,129},{129,193},{2,66},{66,130... | collective-permute-start | bytes 1572872 | tf_op jit(solution)/shard_map/ppermute | solution.py:332
  84.1 14.1 %collective-permute-start.17 = (f32[768,256]{1,0:T(8,128)S(1)}, f32[768,256]{1,0:T(8,128)S(1)}, u32[]{:S(2)}, u32[]{:S(2)}) collective-permute-start(f32[768,256]{1,0:T(8,128)S(1)} %get-tuple-element.209.sent), channel_id=1, source_target_pairs={{1,2},{3,4},{5,6},{7,8},{9,10},{11,12},{13,14},{15,16},{17,18},{19... | collective-permute-start | bytes 2359304 | tf_op jit(solution)/shard_map/ppermute | solution.py:326
  89.2 2.4 %collective-permute-start.15 = (f32[512,256]{1,0:T(8,128)S(1)}, f32[512,256]{1,0:T(8,128)S(1)}, u32[]{:S(2)}, u32[]{:S(2)}) collective-permute-start(f32[512,256]{1,0:T(8,128)S(1)} %get-tuple-element.216), channel_id=1, source_target_pairs={{0,1},{1,0},{2,3},{3,2},{4,5},{5,4},{6,7},{7,6},{8,9},{9,8},{10,11... | collective-permute-start | bytes 1572872 | tf_op jit(solution)/shard_map/ppermute | solution.py:329
  99.5 13.3 %collective-permute-start.20 = (f32[768,256]{1,0:T(8,128)S(1)}, f32[768,256]{1,0:T(8,128)S(1)}, u32[]{:S(2)}, u32[]{:S(2)}) collective-permute-start(f32[768,256]{1,0:T(8,128)S(1)} %get-tuple-element.225.sent), channel_id=1, source_target_pairs={{1,2},{3,4},{5,6},{7,8},{9,10},{11,12},{13,14},{15,16},{17,18},{19... | collective-permute-start | bytes 2359304 | tf_op jit(solution)/shard_map/ppermute | solution.py:326
  103.9 2.4 %collective-permute-start.18 = (f32[512,256]{1,0:T(8,128)S(1)}, f32[512,256]{1,0:T(8,128)S(1)}, u32[]{:S(2)}, u32[]{:S(2)}) collective-permute-start(f32[512,256]{1,0:T(8,128)S(1)} %get-tuple-element.231), channel_id=1, source_target_pairs={{0,1},{1,0},{2,3},{3,2},{4,5},{5,4},{6,7},{7,6},{8,9},{9,8},{10,11... | collective-permute-start | bytes 1572872 | tf_op jit(solution)/shard_map/ppermute | solution.py:329
  114.2 13.3 %collective-permute-start.23 = (f32[768,256]{1,0:T(8,128)S(1)}, f32[768,256]{1,0:T(8,128)S(1)}, u32[]{:S(2)}, u32[]{:S(2)}) collective-permute-start(f32[768,256]{1,0:T(8,128)S(1)} %get-tuple-element.239.sent), channel_id=1, source_target_pairs={{1,2},{3,4},{5,6},{7,8},{9,10},{11,12},{13,14},{15,16},{17,18},{19... | collective-permute-start | bytes 2359304 | tf_op jit(solution)/shard_map/ppermute | solution.py:326
  118.5 2.4 %collective-permute-start.21 = (f32[512,256]{1,0:T(8,128)S(1)}, f32[512,256]{1,0:T(8,128)S(1)}, u32[]{:S(2)}, u32[]{:S(2)}) collective-permute-start(f32[512,256]{1,0:T(8,128)S(1)} %get-tuple-element.245), channel_id=1, source_target_pairs={{0,1},{1,0},{2,3},{3,2},{4,5},{5,4},{6,7},{7,6},{8,9},{9,8},{10,11... | collective-permute-start | bytes 1572872 | tf_op jit(solution)/shard_map/ppermute | solution.py:329
  118.7 2.3 %collective-permute-start.22 = (f32[256,256]{1,0:T(8,128)S(1)}, f32[256,256]{1,0:T(8,128)S(1)}, u32[]{:S(2)}, u32[]{:S(2)}) collective-permute-start(f32[256,256]{1,0:T(8,128)S(1)} %get-tuple-element.246), channel_id=1, source_target_pairs={{0,1},{1,0},{2,3},{3,2},{4,5},{5,4},{6,7},{7,6},{8,9},{9,8},{10,11... | collective-permute-start | bytes 786440 | tf_op jit(solution)/shard_map/ppermute | solution.py:329
  128.8 13.3 %collective-permute-start.26 = (f32[768,256]{1,0:T(8,128)S(1)}, f32[768,256]{1,0:T(8,128)S(1)}, u32[]{:S(2)}, u32[]{:S(2)}) collective-permute-start(f32[768,256]{1,0:T(8,128)S(1)} %get-tuple-element.253.sent), channel_id=1, source_target_pairs={{1,2},{3,4},{5,6},{7,8},{9,10},{11,12},{13,14},{15,16},{17,18},{19... | collective-permute-start | bytes 2359304 | tf_op jit(solution)/shard_map/ppermute | solution.py:326
  133.2 2.9 %collective-permute-start.24 = (f32[512,256]{1,0:T(8,128)S(1)}, f32[512,256]{1,0:T(8,128)S(1)}, u32[]{:S(2)}, u32[]{:S(2)}) collective-permute-start(f32[512,256]{1,0:T(8,128)S(1)} %get-tuple-element.259), channel_id=1, source_target_pairs={{0,1},{1,0},{2,3},{3,2},{4,5},{5,4},{6,7},{7,6},{8,9},{9,8},{10,11... | collective-permute-start | bytes 1572872 | tf_op jit(solution)/shard_map/ppermute | solution.py:329
  133.3 2.8 %collective-permute-start.25 = (f32[256,256]{1,0:T(8,128)S(1)}, f32[256,256]{1,0:T(8,128)S(1)}, u32[]{:S(2)}, u32[]{:S(2)}) collective-permute-start(f32[256,256]{1,0:T(8,128)S(1)} %get-tuple-element.260), channel_id=1, source_target_pairs={{0,1},{1,0},{2,3},{3,2},{4,5},{5,4},{6,7},{7,6},{8,9},{9,8},{10,11... | collective-permute-start | bytes 786440 | tf_op jit(solution)/shard_map/ppermute | solution.py:329
  202.8 5.7 %collective-permute-start.28 = (f32[512,256]{1,0:T(8,128)S(1)}, f32[512,256]{1,0:T(8,128)S(1)}, u32[]{:S(2)}, u32[]{:S(2)}) collective-permute-start(f32[512,256]{1,0:T(8,128)S(1)} %bitcast.23), channel_id=1, source_target_pairs={{0,1},{1,0},{2,3},{3,2},{4,5},{5,4},{6,7},{7,6},{8,9},{9,8},{10,11... | collective-permute-start | bytes 1572872 | tf_op jit(solution)/shard_map/ppermute | solution.py:329
  (18 other events, 91.4 us)

commit v2 on v1

--- a/solution.py
+++ b/solution.py
@@ -64,7 +64,7 @@
     return array, pl.BlockSpec((N, N), lambda i: (0, j))
 
 
-def run(kernel, outs, *operands, flops=0, scratch=()):
+def run(kernel, outs, *operands, flops=0, scratch=(), limit=12):
     arrays, specs = [], []
     for o in operands:
         pair = isinstance(o, tuple)
@@ -77,7 +77,7 @@
         in_specs=specs,
         out_specs=[pl.BlockSpec(memory_space=pltpu.VMEM)] * len(outs),
         scratch_shapes=list(scratch),
-        compiler_params=pltpu.CompilerParams(vmem_limit_bytes=12 << 20),
+        compiler_params=pltpu.CompilerParams(vmem_limit_bytes=limit << 20),
         cost_estimate=pl.CostEstimate(flops=flops, bytes_accessed=1024, transcendentals=0),
     )(*arrays)
 
@@ -90,11 +90,38 @@
 PRODUCT = 1024
 
 
-def band_kernel(tiles, cols, band, across, acc):
+def first_kernel(
+    l, tiles_at, cols_at, y_at, g_at, x_at, gain_second, weight_second_at, gain_first,
+    weight_first_at, band, across, sent, acc, tiles, cols, values, sems,
+):
+    copies = [
+        pltpu.make_async_copy(source, target, sems.at[i])
+        for i, (source, target) in enumerate(
+            [
+                (weight_second_at.at[l], values.at[0]),
+                (y_at.at[:, pl.ds(0, N)], values.at[1]),
+                (weight_first_at.at[0], values.at[2]),
+                (x_at.at[:, pl.ds(N, N)], values.at[3]),
+                (g_at.at[:, pl.ds(N, N)], values.at[4]),
+                (cols_at, cols),
+                (tiles_at, tiles),
+            ]
+        )
+    ]
+    for copy in copies:
+        copy.start()
+    acc[...] = jnp.zeros_like(acc)
+    for copy in copies[:4]:
+        copy.wait()
+    act = active(values[1], gain_second[l : l + 1, :])
+    sent[A, :] = dot6(split3(act), split3(values[0]))
+    act = active(values[3], gain_first[0:1, :])
+    sent[C, :] = dot3(split(act), split(values[2]))
+    for copy in copies[4:]:
+        copy.wait()
     dom = lax.axis_index("dom")
     parity = lax.rem(dom, 2)
     first = (dom - 1) * 2
-    acc[...] = jnp.zeros_like(acc)
     for r in range(2):
         for t in range(TILES):
             place = cols[r, t] - first
@@ -111,6 +138,7 @@
                 band[i, rows, columns] = piece
             for i, piece in enumerate(split(block.T)):
                 across[i, columns, rows] = piece
+    sent[B, :] = owed_to(across, C, values[4])
 
 
 def weight_kernel(first, second, gain_first, gain_second, gains, weights, turned):
@@ -160,14 +188,6 @@
 def weight_grad(k, xhat, back, gains):
     act = jnp.maximum(xhat * gains[k : k + 1, :], 0.0)
     return dot3(split(act.T), split(back))
-
-
-def entry_kernel(l, y1, g2, x2, across, gain_second, weight_second, gain_first, weight_first, sent):
-    act = active(y1[...], gain_second[l : l + 1, :])
-    sent[A, :] = dot6(split3(act), split3(weight_second[l]))
-    sent[B, :] = owed_to(across, C, g2[...])
-    act = active(x2[...], gain_first[0:1, :])
-    sent[C, :] = dot3(split(act), split(weight_first[0]))
 
 
 def next_kernel(
@@ -335,14 +355,6 @@
         return lax.ppermute(v, "segment", [(i + 1, i) for i in range(last)])
 
     part = functools.partial
-    band, across = run(
-        band_kernel,
-        [((3, N, 3 * N), BF16), ((2, 3 * N, N), BF16)],
-        adj_tiles,
-        (tile_cols, pl.BlockSpec(memory_space=pltpu.SMEM)),
-        scratch=[pltpu.VMEM((12, BLOCK, BLOCK), F32)],
-        flops=PRODUCT,
-    )
     gains, weights, turned = run(
         weight_kernel,
         [((2 * LAYERS, N), F32), ((3, 2 * LAYERS, N, N), BF16), ((2, 2 * LAYERS, N, N), BF16)],
@@ -351,10 +363,22 @@
     out, cot, held = back_outputs[0], back_cotangents[0], forward_held[0]
     y1, y2, g1, g2 = half(out, 0), half(out, 1), half(cot, 0), half(cot, 1)
     x1, x2 = half(held, 0), half(held, 1)
-    sent = run(
-        part(entry_kernel, top_layer), [PACK], y1, g2, x2, across, gain_second, weight_second,
-        gain_first, weight_first, flops=3 * PRODUCT,
-    )[0]
+    hbm = pl.BlockSpec(memory_space=pl.ANY)
+    band, across, sent = run(
+        part(first_kernel, top_layer),
+        [((3, N, 3 * N), BF16), ((2, 3 * N, N), BF16), PACK],
+        (adj_tiles, hbm), (tile_cols, hbm), (out, hbm), (cot, hbm), (held, hbm), gain_second,
+        (weight_second, hbm), gain_first, (weight_first, hbm),
+        scratch=[
+            pltpu.VMEM((12, BLOCK, BLOCK), F32),
+            pltpu.VMEM((2, TILES, BLOCK, BLOCK), F32),
+            pltpu.SMEM((2, TILES), jnp.int32),
+            pltpu.VMEM((5, N, N), F32),
+            pltpu.SemaphoreType.DMA((7,)),
+        ],
+        flops=PRODUCT,
+        limit=54,
+    )
     grads, results = {}, []
     for slot in range(2):
         for step in range(2 * LAYERS):

time: 210 us -> 210 us (level)
  waiting for transfers between devices: 71.7 us -> 68.4 us
  Pallas kernels: 28.3 us -> 31.3 us
    ppermute x8, waiting for transfers between devices: 47.9 us -> 44.6 us  [far(): return lax.ppermute(v, 'dom', far_pairs)]
    pallas_call x39 -> x38, Pallas kernels: 28.3 us -> 31.3 us  [run(): pl.pallas_call(kernel, out_shape=[jax.ShapeDtypeStruct(s, t) for s, t in...]
where the time goes in v2:
time: 210 us; the launch traced here: 209 us
  waiting for transfers between devices  68.4 us (33%)
  blocking collectives  58.2 us (28%)
  starting transfers between devices  46.7 us (22%)
  Pallas kernels  31.3 us (15%)
  local copies, waits for them, and re-layouts  3.58 us (2%)
    all_to_all x2, blocking collectives, exchanged(): return lax.all_to_all(v, 'dom', 0, 0, axis_index_groups=groups, tiled=True)  58.2 us
    ppermute x8, waiting for transfers between devices, far(): return lax.ppermute(v, 'dom', far_pairs)  44.6 us
    ppermute x8, starting transfers between devices, far(): return lax.ppermute(v, 'dom', far_pairs)  31.3 us
    pallas_call x38, Pallas kernels, run(): pl.pallas_call(kernel, out_shape=[jax.ShapeDtypeStruct(s, t) for s, t in...  31.3 us
    ppermute x18, waiting for transfers between devices, near(): return lax.ppermute(v, 'dom', sib_pairs)  12.7 us
    ppermute x2, waiting for transfers between devices, backward(): return lax.ppermute(v, 'segment', [(i + 1, i) for i in range(last)])  11.1 us
    ppermute x18, starting transfers between devices, near(): return lax.ppermute(v, 'dom', sib_pairs)  8.84 us
  transfers between devices with their start and end apart: 29, of which 17 were waited for; matrix products, arithmetic and copies ran while one was open for 0% of the time, Pallas kernels for 8%

profile of v2, /device:TPU:1, one launch (start us, length us, event | category | flops | bytes accessed | tf_op | source)
XLA Modules:
  0.0 209.4 jit_solution(16139849716511054422)
XLA Ops:
  0.7 5.0 %shard_map.195 = (bf16[3,256,768]{2,1,0:T(8,128)(2,1)}, bf16[2,768,256]{2,1,0:T(8,128)(2,1)}, f32[768,256]{1,0:T(8,128)}) custom-call(f32[2,16,128,128]{3,2,1,0:T(8,128)} %tiles_at.1, s32[2,16]{1,0:T(2,128)} %cols_at.1, f32[256,512]{1,0:T(8,128)} %bitcast.15, f32[256,512]{1,0:T(8,128)} %bitcast.11, f32[256,512]{1,0:T(8,128)} %bitcast.19, ...), custom_call_target="tpu_custom_call" | custom-call | flops 1024 | bytes 1024 | tf_op jit(solution)/shard_map/pallas_call | solution.py:73
  5.7 4.9 %collective-permute-start.2 = (f32[768,256]{1,0:T(8,128)}, f32[768,256]{1,0:T(8,128)S(1)}, u32[]{:S(2)}, u32[]{:S(2)}) collective-permute-start(f32[768,256]{1,0:T(8,128)} %get-tuple-element.149.sent), channel_id=1, source_target_pairs={{1,2},{3,4},{5,6},{7,8},{9,10},{11,12},{13,14},{15,16},{17,18},{19... | collective-permute-start | bytes 2359304 | tf_op jit(solution)/shard_map/ppermute | solution.py:346
  17.9 2.7 %collective-permute-done.2.far = f32[768,256]{1,0:T(8,128)S(1)} collective-permute-done((f32[768,256]{1,0:T(8,128)}, f32[768,256]{1,0:T(8,128)S(1)}, u32[]{:S(2)}, u32[]{:S(2)}) %collective-permute-start.2) | collective-permute-done | bytes 786464 | tf_op jit(solution)/shard_map/ppermute | solution.py:346
  21.9 3.6 %collective-permute-start.5 = (f32[768,256]{1,0:T(8,128)S(1)}, f32[768,256]{1,0:T(8,128)S(1)}, u32[]{:S(2)}, u32[]{:S(2)}) collective-permute-start(f32[768,256]{1,0:T(8,128)S(1)} %get-tuple-element.165.sent), channel_id=1, source_target_pairs={{1,2},{3,4},{5,6},{7,8},{9,10},{11,12},{13,14},{15,16},{17,18},{19... | collective-permute-start | bytes 2359304 | tf_op jit(solution)/shard_map/ppermute | solution.py:346
  26.8 1.8 collective-permute-done.4.near_owed
  29.1 6.1 %collective-permute-done.5.far = f32[768,256]{1,0:T(8,128)S(1)} collective-permute-done((f32[768,256]{1,0:T(8,128)S(1)}, f32[768,256]{1,0:T(8,128)S(1)}, u32[]{:S(2)}, u32[]{:S(2)}) %collective-permute-start.5) | collective-permute-done | bytes 786464 | tf_op jit(solution)/shard_map/ppermute | solution.py:346
  36.6 3.6 %collective-permute-start.8 = (f32[768,256]{1,0:T(8,128)S(1)}, f32[768,256]{1,0:T(8,128)S(1)}, u32[]{:S(2)}, u32[]{:S(2)}) collective-permute-start(f32[768,256]{1,0:T(8,128)S(1)} %get-tuple-element.178.sent), channel_id=1, source_target_pairs={{1,2},{3,4},{5,6},{7,8},{9,10},{11,12},{13,14},{15,16},{17,18},{19... | collective-permute-start | bytes 2359304 | tf_op jit(solution)/shard_map/ppermute | solution.py:346
  43.8 6.0 %collective-permute-done.8.far = f32[768,256]{1,0:T(8,128)S(1)} collective-permute-done((f32[768,256]{1,0:T(8,128)S(1)}, f32[768,256]{1,0:T(8,128)S(1)}, u32[]{:S(2)}, u32[]{:S(2)}) %collective-permute-start.8) | collective-permute-done | bytes 786464 | tf_op jit(solution)/shard_map/ppermute | solution.py:346
  51.2 3.8 %collective-permute-start.11 = (f32[768,256]{1,0:T(8,128)S(1)}, f32[768,256]{1,0:T(8,128)S(1)}, u32[]{:S(2)}, u32[]{:S(2)}) collective-permute-start(f32[768,256]{1,0:T(8,128)S(1)} %get-tuple-element.192.sent), channel_id=1, source_target_pairs={{1,2},{3,4},{5,6},{7,8},{9,10},{11,12},{13,14},{15,16},{17,18},{19... | collective-permute-start | bytes 2359304 | tf_op jit(solution)/shard_map/ppermute | solution.py:346
  58.7 6.2 %collective-permute-done.11.far = f32[768,256]{1,0:T(8,128)S(1)} collective-permute-done((f32[768,256]{1,0:T(8,128)S(1)}, f32[768,256]{1,0:T(8,128)S(1)}, u32[]{:S(2)}, u32[]{:S(2)}) %collective-permute-start.11) | collective-permute-done | bytes 786464 | tf_op jit(solution)/shard_map/ppermute | solution.py:346
  67.8 4.0 %collective-permute-start.14 = (f32[512,256]{1,0:T(8,128)S(1)}, f32[512,256]{1,0:T(8,128)S(1)}, u32[]{:S(2)}, u32[]{:S(2)}) collective-permute-start(f32[512,256]{1,0:T(8,128)S(1)} %get-tuple-element.210), channel_id=1, source_target_pairs={{0,64},{64,128},{128,192},{1,65},{65,129},{129,193},{2,66},{66,130... | collective-permute-start | bytes 1572872 | tf_op jit(solution)/shard_map/ppermute | solution.py:352
  71.9 11.1 %collective-permute-done.13.late = f32[512,256]{1,0:T(8,128)S(1)} collective-permute-done((f32[512,256]{1,0:T(8,128)S(1)}, f32[512,256]{1,0:T(8,128)S(1)}, u32[]{:S(2)}, u32[]{:S(2)}) %collective-permute-start.13) | collective-permute-done | bytes 524320 | tf_op jit(solution)/shard_map/ppermute | solution.py:355
  83.8 4.4 %collective-permute-start.17 = (f32[768,256]{1,0:T(8,128)S(1)}, f32[768,256]{1,0:T(8,128)S(1)}, u32[]{:S(2)}, u32[]{:S(2)}) collective-permute-start(f32[768,256]{1,0:T(8,128)S(1)} %get-tuple-element.211.sent), channel_id=1, source_target_pairs={{1,2},{3,4},{5,6},{7,8},{9,10},{11,12},{13,14},{15,16},{17,18},{19... | collective-permute-start | bytes 2359304 | tf_op jit(solution)/shard_map/ppermute | solution.py:346
  91.8 6.1 %collective-permute-done.17.far = f32[768,256]{1,0:T(8,128)S(1)} collective-permute-done((f32[768,256]{1,0:T(8,128)S(1)}, f32[768,256]{1,0:T(8,128)S(1)}, u32[]{:S(2)}, u32[]{:S(2)}) %collective-permute-start.17) | collective-permute-done | bytes 786464 | tf_op jit(solution)/shard_map/ppermute | solution.py:346
  99.2 3.6 %collective-permute-start.20 = (f32[768,256]{1,0:T(8,128)S(1)}, f32[768,256]{1,0:T(8,128)S(1)}, u32[]{:S(2)}, u32[]{:S(2)}) collective-permute-start(f32[768,256]{1,0:T(8,128)S(1)} %get-tuple-element.227.sent), channel_id=1, source_target_pairs={{1,2},{3,4},{5,6},{7,8},{9,10},{11,12},{13,14},{15,16},{17,18},{19... | collective-permute-start | bytes 2359304 | tf_op jit(solution)/shard_map/ppermute | solution.py:346
  106.5 6.0 %collective-permute-done.20.far = f32[768,256]{1,0:T(8,128)S(1)} collective-permute-done((f32[768,256]{1,0:T(8,128)S(1)}, f32[768,256]{1,0:T(8,128)S(1)}, u32[]{:S(2)}, u32[]{:S(2)}) %collective-permute-start.20) | collective-permute-done | bytes 786464 | tf_op jit(solution)/shard_map/ppermute | solution.py:346
  113.9 3.6 %collective-permute-start.23 = (f32[768,256]{1,0:T(8,128)S(1)}, f32[768,256]{1,0:T(8,128)S(1)}, u32[]{:S(2)}, u32[]{:S(2)}) collective-permute-start(f32[768,256]{1,0:T(8,128)S(1)} %get-tuple-element.241.sent), channel_id=1, source_target_pairs={{1,2},{3,4},{5,6},{7,8},{9,10},{11,12},{13,14},{15,16},{17,18},{19... | collective-permute-start | bytes 2359304 | tf_op jit(solution)/shard_map/ppermute | solution.py:346
  121.1 6.1 %collective-permute-done.23.far = f32[768,256]{1,0:T(8,128)S(1)} collective-permute-done((f32[768,256]{1,0:T(8,128)S(1)}, f32[768,256]{1,0:T(8,128)S(1)}, u32[]{:S(2)}, u32[]{:S(2)}) %collective-permute-start.23) | collective-permute-done | bytes 786464 | tf_op jit(solution)/shard_map/ppermute | solution.py:346
  128.5 3.6 %collective-permute-start.26 = (f32[768,256]{1,0:T(8,128)S(1)}, f32[768,256]{1,0:T(8,128)S(1)}, u32[]{:S(2)}, u32[]{:S(2)}) collective-permute-start(f32[768,256]{1,0:T(8,128)S(1)} %get-tuple-element.255.sent), channel_id=1, source_target_pairs={{1,2},{3,4},{5,6},{7,8},{9,10},{11,12},{13,14},{15,16},{17,18},{19... | collective-permute-start | bytes 2359304 | tf_op jit(solution)/shard_map/ppermute | solution.py:346
  136.3 5.5 %collective-permute-done.26.far = f32[768,256]{1,0:T(8,128)S(1)} collective-permute-done((f32[768,256]{1,0:T(8,128)S(1)}, f32[768,256]{1,0:T(8,128)S(1)}, u32[]{:S(2)}, u32[]{:S(2)}) %collective-permute-start.26) | collective-permute-done | bytes 786464 | tf_op jit(solution)/shard_map/ppermute | solution.py:346
  142.3 1.9 collective-permute-done.27.b
  144.2 36.2 %all_to_all.10.parts = f32[32,16,256]{2,1,0:T(8,128)S(1)} all-to-all(f32[32,16,256]{2,1,0:T(8,128)S(1)} %bitcast.22), channel_id=1, replica_groups={{0,2,4,6,8,10,12,14,16,18,20,22,24,26,28,30,32,34,36,38,40,42,44,46,48,..., dimensions={0} | all-to-all | bytes 1048576 | tf_op jit(solution)/shard_map/all_to_all | solution.py:446
  180.6 22.0 %all_to_all.11 = f32[32,16,256]{2,1,0:T(8,128)S(1)} all-to-all(f32[32,16,256]{2,1,0:T(8,128)S(1)} %shard_map.231), channel_id=1, replica_groups={{0,2,4,6,8,10,12,14,16,18,20,22,24,26,28,30,32,34,36,38,40,42,44,46,48,..., dimensions={0} | all-to-all | bytes 1048576 | tf_op jit(solution)/shard_map/all_to_all | solution.py:446
  202.5 4.0 %collective-permute-start.28 = (f32[512,256]{1,0:T(8,128)S(1)}, f32[512,256]{1,0:T(8,128)S(1)}, u32[]{:S(2)}, u32[]{:S(2)}) collective-permute-start(f32[512,256]{1,0:T(8,128)S(1)} %bitcast.23), channel_id=1, source_target_pairs={{0,1},{1,0},{2,3},{3,2},{4,5},{5,4},{6,7},{7,6},{8,9},{9,8},{10,11... | collective-permute-start | bytes 1572872 | tf_op jit(solution)/shard_map/ppermute | solution.py:349
  (104 shorter events, 46.2 us)
Async XLA Ops:
  5.7 14.8 %collective-permute-start.2 = (f32[768,256]{1,0:T(8,128)}, f32[768,256]{1,0:T(8,128)S(1)}, u32[]{:S(2)}, u32[]{:S(2)}) collective-permute-start(f32[768,256]{1,0:T(8,128)} %get-tuple-element.149.sent), channel_id=1, source_target_pairs={{1,2},{3,4},{5,6},{7,8},{9,10},{11,12},{13,14},{15,16},{17,18},{19... | collective-permute-start | bytes 2359304 | tf_op jit(solution)/shard_map/ppermute | solution.py:346
  15.0 2.4 %collective-permute-start = (f32[512,256]{1,0:T(8,128)S(1)}, f32[512,256]{1,0:T(8,128)S(1)}, u32[]{:S(2)}, u32[]{:S(2)}) collective-permute-start(f32[512,256]{1,0:T(8,128)S(1)} %get-tuple-element.155), channel_id=1, source_target_pairs={{0,1},{1,0},{2,3},{3,2},{4,5},{5,4},{6,7},{7,6},{8,9},{9,8},{10,11... | collective-permute-start | bytes 1572872 | tf_op jit(solution)/shard_map/ppermute | solution.py:349
  15.1 2.3 %collective-permute-start.1 = (f32[256,256]{1,0:T(8,128)S(1)}, f32[256,256]{1,0:T(8,128)S(1)}, u32[]{:S(2)}, u32[]{:S(2)}) collective-permute-start(f32[256,256]{1,0:T(8,128)S(1)} %get-tuple-element.156), channel_id=1, source_target_pairs={{0,1},{1,0},{2,3},{3,2},{4,5},{5,4},{6,7},{7,6},{8,9},{9,8},{10,11... | collective-permute-start | bytes 786440 | tf_op jit(solution)/shard_map/ppermute | solution.py:349
  21.9 13.3 %collective-permute-start.5 = (f32[768,256]{1,0:T(8,128)S(1)}, f32[768,256]{1,0:T(8,128)S(1)}, u32[]{:S(2)}, u32[]{:S(2)}) collective-permute-start(f32[768,256]{1,0:T(8,128)S(1)} %get-tuple-element.165.sent), channel_id=1, source_target_pairs={{1,2},{3,4},{5,6},{7,8},{9,10},{11,12},{13,14},{15,16},{17,18},{19... | collective-permute-start | bytes 2359304 | tf_op jit(solution)/shard_map/ppermute | solution.py:346
  26.2 2.4 %collective-permute-start.3 = (f32[512,256]{1,0:T(8,128)S(1)}, f32[512,256]{1,0:T(8,128)S(1)}, u32[]{:S(2)}, u32[]{:S(2)}) collective-permute-start(f32[512,256]{1,0:T(8,128)S(1)} %get-tuple-element.170), channel_id=1, source_target_pairs={{0,1},{1,0},{2,3},{3,2},{4,5},{5,4},{6,7},{7,6},{8,9},{9,8},{10,11... | collective-permute-start | bytes 1572872 | tf_op jit(solution)/shard_map/ppermute | solution.py:349
  36.6 13.3 %collective-permute-start.8 = (f32[768,256]{1,0:T(8,128)S(1)}, f32[768,256]{1,0:T(8,128)S(1)}, u32[]{:S(2)}, u32[]{:S(2)}) collective-permute-start(f32[768,256]{1,0:T(8,128)S(1)} %get-tuple-element.178.sent), channel_id=1, source_target_pairs={{1,2},{3,4},{5,6},{7,8},{9,10},{11,12},{13,14},{15,16},{17,18},{19... | collective-permute-start | bytes 2359304 | tf_op jit(solution)/shard_map/ppermute | solution.py:346
  40.9 2.4 %collective-permute-start.6 = (f32[512,256]{1,0:T(8,128)S(1)}, f32[512,256]{1,0:T(8,128)S(1)}, u32[]{:S(2)}, u32[]{:S(2)}) collective-permute-start(f32[512,256]{1,0:T(8,128)S(1)} %get-tuple-element.184), channel_id=1, source_target_pairs={{0,1},{1,0},{2,3},{3,2},{4,5},{5,4},{6,7},{7,6},{8,9},{9,8},{10,11... | collective-permute-start | bytes 1572872 | tf_op jit(solution)/shard_map/ppermute | solution.py:349
  41.0 2.3 %collective-permute-start.7 = (f32[256,256]{1,0:T(8,128)S(1)}, f32[256,256]{1,0:T(8,128)S(1)}, u32[]{:S(2)}, u32[]{:S(2)}) collective-permute-start(f32[256,256]{1,0:T(8,128)S(1)} %get-tuple-element.185), channel_id=1, source_target_pairs={{0,1},{1,0},{2,3},{3,2},{4,5},{5,4},{6,7},{7,6},{8,9},{9,8},{10,11... | collective-permute-start | bytes 786440 | tf_op jit(solution)/shard_map/ppermute | solution.py:349
  51.2 13.6 %collective-permute-start.11 = (f32[768,256]{1,0:T(8,128)S(1)}, f32[768,256]{1,0:T(8,128)S(1)}, u32[]{:S(2)}, u32[]{:S(2)}) collective-permute-start(f32[768,256]{1,0:T(8,128)S(1)} %get-tuple-element.192.sent), channel_id=1, source_target_pairs={{1,2},{3,4},{5,6},{7,8},{9,10},{11,12},{13,14},{15,16},{17,18},{19... | collective-permute-start | bytes 2359304 | tf_op jit(solution)/shard_map/ppermute | solution.py:346
  55.8 2.4 %collective-permute-start.9 = (f32[512,256]{1,0:T(8,128)S(1)}, f32[512,256]{1,0:T(8,128)S(1)}, u32[]{:S(2)}, u32[]{:S(2)}) collective-permute-start(f32[512,256]{1,0:T(8,128)S(1)} %get-tuple-element.198), channel_id=1, source_target_pairs={{0,1},{1,0},{2,3},{3,2},{4,5},{5,4},{6,7},{7,6},{8,9},{9,8},{10,11... | collective-permute-start | bytes 1572872 | tf_op jit(solution)/shard_map/ppermute | solution.py:349
  56.4 15.5 %collective-permute-start.12 = (f32[512,256]{1,0:T(8,128)S(1)}, f32[512,256]{1,0:T(8,128)S(1)}, u32[]{:S(2)}, u32[]{:S(2)}) collective-permute-start(f32[512,256]{1,0:T(8,128)S(1)} %get-tuple-element.208), channel_id=1, source_target_pairs={{64,0},{128,64},{192,128},{65,1},{129,65},{193,129},{66,2},{130,66... | collective-permute-start | bytes 1572872 | tf_op jit(solution)/shard_map/ppermute | solution.py:355
  66.5 16.4 %collective-permute-start.13 = (f32[512,256]{1,0:T(8,128)S(1)}, f32[512,256]{1,0:T(8,128)S(1)}, u32[]{:S(2)}, u32[]{:S(2)}) collective-permute-start(f32[512,256]{1,0:T(8,128)S(1)} %get-tuple-element.209), channel_id=1, source_target_pairs={{64,0},{128,64},{192,128},{65,1},{129,65},{193,129},{66,2},{130,66... | collective-permute-start | bytes 1572872 | tf_op jit(solution)/shard_map/ppermute | solution.py:355
  67.8 15.1 %collective-permute-start.14 = (f32[512,256]{1,0:T(8,128)S(1)}, f32[512,256]{1,0:T(8,128)S(1)}, u32[]{:S(2)}, u32[]{:S(2)}) collective-permute-start(f32[512,256]{1,0:T(8,128)S(1)} %get-tuple-element.210), channel_id=1, source_target_pairs={{0,64},{64,128},{128,192},{1,65},{65,129},{129,193},{2,66},{66,130... | collective-permute-start | bytes 1572872 | tf_op jit(solution)/shard_map/ppermute | solution.py:352
  83.8 14.1 %collective-permute-start.17 = (f32[768,256]{1,0:T(8,128)S(1)}, f32[768,256]{1,0:T(8,128)S(1)}, u32[]{:S(2)}, u32[]{:S(2)}) collective-permute-start(f32[768,256]{1,0:T(8,128)S(1)} %get-tuple-element.211.sent), channel_id=1, source_target_pairs={{1,2},{3,4},{5,6},{7,8},{9,10},{11,12},{13,14},{15,16},{17,18},{19... | collective-permute-start | bytes 2359304 | tf_op jit(solution)/shard_map/ppermute | solution.py:346
  88.9 2.4 %collective-permute-start.15 = (f32[512,256]{1,0:T(8,128)S(1)}, f32[512,256]{1,0:T(8,128)S(1)}, u32[]{:S(2)}, u32[]{:S(2)}) collective-permute-start(f32[512,256]{1,0:T(8,128)S(1)} %get-tuple-element.218), channel_id=1, source_target_pairs={{0,1},{1,0},{2,3},{3,2},{4,5},{5,4},{6,7},{7,6},{8,9},{9,8},{10,11... | collective-permute-start | bytes 1572872 | tf_op jit(solution)/shard_map/ppermute | solution.py:349
  99.2 13.3 %collective-permute-start.20 = (f32[768,256]{1,0:T(8,128)S(1)}, f32[768,256]{1,0:T(8,128)S(1)}, u32[]{:S(2)}, u32[]{:S(2)}) collective-permute-start(f32[768,256]{1,0:T(8,128)S(1)} %get-tuple-element.227.sent), channel_id=1, source_target_pairs={{1,2},{3,4},{5,6},{7,8},{9,10},{11,12},{13,14},{15,16},{17,18},{19... | collective-permute-start | bytes 2359304 | tf_op jit(solution)/shard_map/ppermute | solution.py:346
  103.6 2.4 %collective-permute-start.18 = (f32[512,256]{1,0:T(8,128)S(1)}, f32[512,256]{1,0:T(8,128)S(1)}, u32[]{:S(2)}, u32[]{:S(2)}) collective-permute-start(f32[512,256]{1,0:T(8,128)S(1)} %get-tuple-element.233), channel_id=1, source_target_pairs={{0,1},{1,0},{2,3},{3,2},{4,5},{5,4},{6,7},{7,6},{8,9},{9,8},{10,11... | collective-permute-start | bytes 1572872 | tf_op jit(solution)/shard_map/ppermute | solution.py:349
  113.9 13.3 %collective-permute-start.23 = (f32[768,256]{1,0:T(8,128)S(1)}, f32[768,256]{1,0:T(8,128)S(1)}, u32[]{:S(2)}, u32[]{:S(2)}) collective-permute-start(f32[768,256]{1,0:T(8,128)S(1)} %get-tuple-element.241.sent), channel_id=1, source_target_pairs={{1,2},{3,4},{5,6},{7,8},{9,10},{11,12},{13,14},{15,16},{17,18},{19... | collective-permute-start | bytes 2359304 | tf_op jit(solution)/shard_map/ppermute | solution.py:346
  118.2 2.4 %collective-permute-start.21 = (f32[512,256]{1,0:T(8,128)S(1)}, f32[512,256]{1,0:T(8,128)S(1)}, u32[]{:S(2)}, u32[]{:S(2)}) collective-permute-start(f32[512,256]{1,0:T(8,128)S(1)} %get-tuple-element.247), channel_id=1, source_target_pairs={{0,1},{1,0},{2,3},{3,2},{4,5},{5,4},{6,7},{7,6},{8,9},{9,8},{10,11... | collective-permute-start | bytes 1572872 | tf_op jit(solution)/shard_map/ppermute | solution.py:349
  118.3 2.3 %collective-permute-start.22 = (f32[256,256]{1,0:T(8,128)S(1)}, f32[256,256]{1,0:T(8,128)S(1)}, u32[]{:S(2)}, u32[]{:S(2)}) collective-permute-start(f32[256,256]{1,0:T(8,128)S(1)} %get-tuple-element.248), channel_id=1, source_target_pairs={{0,1},{1,0},{2,3},{3,2},{4,5},{5,4},{6,7},{7,6},{8,9},{9,8},{10,11... | collective-permute-start | bytes 786440 | tf_op jit(solution)/shard_map/ppermute | solution.py:349
  128.5 13.3 %collective-permute-start.26 = (f32[768,256]{1,0:T(8,128)S(1)}, f32[768,256]{1,0:T(8,128)S(1)}, u32[]{:S(2)}, u32[]{:S(2)}) collective-permute-start(f32[768,256]{1,0:T(8,128)S(1)} %get-tuple-element.255.sent), channel_id=1, source_target_pairs={{1,2},{3,4},{5,6},{7,8},{9,10},{11,12},{13,14},{15,16},{17,18},{19... | collective-permute-start | bytes 2359304 | tf_op jit(solution)/shard_map/ppermute | solution.py:346
  132.9 2.9 %collective-permute-start.24 = (f32[512,256]{1,0:T(8,128)S(1)}, f32[512,256]{1,0:T(8,128)S(1)}, u32[]{:S(2)}, u32[]{:S(2)}) collective-permute-start(f32[512,256]{1,0:T(8,128)S(1)} %get-tuple-element.261), channel_id=1, source_target_pairs={{0,1},{1,0},{2,3},{3,2},{4,5},{5,4},{6,7},{7,6},{8,9},{9,8},{10,11... | collective-permute-start | bytes 1572872 | tf_op jit(solution)/shard_map/ppermute | solution.py:349
  133.0 2.8 %collective-permute-start.25 = (f32[256,256]{1,0:T(8,128)S(1)}, f32[256,256]{1,0:T(8,128)S(1)}, u32[]{:S(2)}, u32[]{:S(2)}) collective-permute-start(f32[256,256]{1,0:T(8,128)S(1)} %get-tuple-element.262), channel_id=1, source_target_pairs={{0,1},{1,0},{2,3},{3,2},{4,5},{5,4},{6,7},{7,6},{8,9},{9,8},{10,11... | collective-permute-start | bytes 786440 | tf_op jit(solution)/shard_map/ppermute | solution.py:349
  202.5 5.7 %collective-permute-start.28 = (f32[512,256]{1,0:T(8,128)S(1)}, f32[512,256]{1,0:T(8,128)S(1)}, u32[]{:S(2)}, u32[]{:S(2)}) collective-permute-start(f32[512,256]{1,0:T(8,128)S(1)} %bitcast.23), channel_id=1, source_target_pairs={{0,1},{1,0},{2,3},{3,2},{4,5},{5,4},{6,7},{7,6},{8,9},{9,8},{10,11... | collective-permute-start | bytes 1572872 | tf_op jit(solution)/shard_map/ppermute | solution.py:349
  (20 other events, 110.7 us)
